TPU v7x, 256 devices: a whole 4x4x8 slice. The times are simulated.
256 devices in a mesh: dp: 16 (over z, core), tensor: 16 (over y, x).
Axes of the slice: x: 4, y: 4, z: 8, core: 2. Of those that a mesh axis runs over, the one named last changes fastest.
Arguments:
- tokens: bfloat16 [4096, 4096], P('dp'), may hold values from -30 to 30
- neighbour_buffer: bfloat16 [256, 128, 4096], P('dp', None, 'tensor'), may hold values from -6 to 6
- shard_ids: int32 [64, 2], P('dp'), may hold values from 0 to 15, as said below
- row_ids: int32 [64, 2], P('dp'), may hold values from 0 to 15
- query_weight: bfloat16 [4096, 2048], P(None, 'tensor'), may hold values from -0.09375 to 0.09375
- key_weight: bfloat16 [4096, 2048], P(None, 'tensor'), may hold values from -0.09375 to 0.09375
- value_weight: bfloat16 [4096, 2048], P(None, 'tensor'), may hold values from -0.09375 to 0.09375
- output_weight: bfloat16 [2048, 4096], P('tensor'), may hold values from -0.5 to 0.5
- up_weight: bfloat16 [4096, 8192], P('dp', 'tensor'), may hold values from -0.09375 to 0.09375
- down_weight: bfloat16 [8192, 4096], P('tensor', 'dp'), may hold values from -0.0625 to 0.0625
- grad_output: bfloat16 [4096, 4096], P('dp'), may hold values from -6 to 6
Outputs:
- layer_out: bfloat16 [4096, 4096], P(('dp', 'tensor'))
- grad_tokens: bfloat16 [4096, 4096], P(('dp', 'tensor'))
- query_grad: float32 [4096, 2048], P('dp', 'tensor')
- key_grad: float32 [4096, 2048], P('dp', 'tensor')
- value_grad: float32 [4096, 2048], P('dp', 'tensor')
- mix_grad: float32 [2048, 4096], P('tensor', 'dp')
Inputs may be any that keep to these rules, and one draw needn't show every extreme that they name: `shard_ids`: A block's two neighbours lie in different shards. Among the 4 blocks of one index of dp no shard is named more than 2 times, and some shard is named exactly 2 times among the blocks of every index of dp.
All inputs are finite; a program needn't handle non-finite values.
Results may differ from a plain program's by a relative error of at most 0.034.
Values may be sent and summed in bfloat16 or wider, within the bound.
No kernel may reach another device: no remote copies, remote signals or barrier semaphores. Data moves between devices by JAX's collectives and lax.ppermute only.
A program may use at most 128 MiB of HBM per device.

v0:
```python
import math

import jax
import jax.numpy as jnp
from jax import lax
from jax.sharding import PartitionSpec as P

HD = 128
BLOCK = 64
NLEN = 128


epsilon = 1e-06
gelu_root = 0.7978845608028654
gelu_cubic = 0.044715


def rms_scale(values):
    return lax.rsqrt(jnp.mean(values * values, axis=-1, keepdims=True) + epsilon)


def norm_back(values, factor, incoming):
    normal_part = values * factor
    return (
        incoming - normal_part * jnp.mean(incoming * normal_part, axis=-1, keepdims=True)
    ) * factor


def gelu_value(inputs):
    inner = gelu_root * (inputs + gelu_cubic * inputs * inputs * inputs)
    return 0.5 * inputs * (1.0 + jnp.tanh(inner))


def gelu_slope(inputs):
    inner = gelu_root * (inputs + gelu_cubic * inputs * inputs * inputs)
    tanh_part = jnp.tanh(inner)
    return 0.5 * (1.0 + tanh_part) + 0.5 * inputs * (1.0 - tanh_part * tanh_part) * gelu_root * (
        1.0 + 3.0 * gelu_cubic * inputs * inputs
    )


def rounded(partial_value):
    return lax.optimization_barrier(partial_value.astype(jnp.bfloat16)).astype(jnp.float32)


def contract_last(left_side, right_side):
    return lax.dot_general(
        left_side, right_side, (((1,), (1,)), ((), ())), preferred_element_type=jnp.float32
    )


def contract_first(left_side, right_side):
    return lax.dot_general(
        left_side, right_side, (((0,), (0,)), ((), ())), preferred_element_type=jnp.float32
    )


def local(
    tokens,
    neighbour_buffer,
    shard_ids,
    row_ids,
    query_weight,
    key_weight,
    value_weight,
    output_weight,
    up_weight,
    down_weight,
    grad_output,
):
    data_size = lax.axis_size("dp")
    tensor_size = lax.axis_size("tensor")
    token_count = tokens.shape[0]
    width = tokens.shape[1]
    block_count = shard_ids.shape[0]
    capacity = block_count // 2
    pair_count = 2 * block_count
    owners = shard_ids.reshape(pair_count)
    wanted = row_ids.reshape(pair_count)
    same_owner = owners[:, None] == owners[None, :]
    earlier = lax.broadcasted_iota(jnp.int32, (pair_count, pair_count), 0) < lax.broadcasted_iota(
        jnp.int32, (pair_count, pair_count), 1
    )
    slot_index = jnp.sum((same_owner & earlier).astype(jnp.int32), axis=0)
    owner_grid = lax.broadcasted_iota(jnp.int32, (data_size, capacity, pair_count), 0)
    slot_grid = lax.broadcasted_iota(jnp.int32, (data_size, capacity, pair_count), 1)
    slot_match = (owners[None, None, :] == owner_grid) & (slot_index[None, None, :] == slot_grid)
    requests = jnp.sum(jnp.where(slot_match, wanted[None, None, :], 0), axis=2)
    replies = lax.all_to_all(
        jnp.take(
            neighbour_buffer,
            lax.all_to_all(requests, "dp", split_axis=0, concat_axis=0, tiled=True),
            axis=0,
        ),
        "dp",
        split_axis=0,
        concat_axis=0,
        tiled=True,
    )
    reply_rows = replies.reshape(data_size * capacity, replies.shape[2], replies.shape[3])
    local_enc = jnp.take(reply_rows, owners * capacity + slot_index, axis=0)
    encodings = lax.all_gather(local_enc, "tensor", axis=2, tiled=True)
    enc_rows = encodings.reshape(pair_count * NLEN, width)
    up_full, down_full = (
        lax.all_gather(up_weight, "dp", axis=0, tiled=True),
        lax.all_gather(down_weight, "dp", axis=1, tiled=True),
    )
    token_f = tokens.astype(jnp.float32)
    base_scale = rms_scale(token_f)
    normed = (token_f * base_scale).astype(jnp.bfloat16)
    query_rows = jnp.dot(normed, query_weight, preferred_element_type=jnp.float32).astype(
        jnp.bfloat16
    )
    key_rows = jnp.dot(enc_rows, key_weight, preferred_element_type=jnp.float32).astype(
        jnp.bfloat16
    )
    value_rows = jnp.dot(enc_rows, value_weight, preferred_element_type=jnp.float32).astype(
        jnp.bfloat16
    )
    head_width = query_rows.shape[1]
    heads_here = head_width // HD
    query_heads = query_rows.reshape(block_count, BLOCK, heads_here, HD)
    key_heads = key_rows.reshape(block_count, 2 * NLEN, heads_here, HD)
    value_heads = value_rows.reshape(block_count, 2 * NLEN, heads_here, HD)
    score_factor = 1.0 / math.sqrt(HD)
    scores = (
        jnp.einsum("cqhd,ckhd->chqk", query_heads, key_heads, preferred_element_type=jnp.float32)
        * score_factor
    )
    raised = jnp.exp(scores)
    attention = raised / jnp.sum(raised, axis=-1, keepdims=True)
    attention_b = attention.astype(jnp.bfloat16)
    head_mix = jnp.einsum(
        "chqk,ckhd->cqhd", attention_b, value_heads, preferred_element_type=jnp.float32
    ).astype(jnp.bfloat16)
    mix_rows = head_mix.reshape(token_count, head_width)
    attn_part = jnp.dot(mix_rows, output_weight, preferred_element_type=jnp.float32)
    rows_share = token_count // tensor_size
    row_start = lax.axis_index("tensor") * rows_share
    token_rows = lax.dynamic_slice_in_dim(token_f, row_start, rows_share, 0)
    base_rows = lax.dynamic_slice_in_dim(base_scale, row_start, rows_share, 0)
    attn_rows = lax.psum_scatter(
        attn_part.astype(jnp.bfloat16), "tensor", scatter_dimension=0, tiled=True
    ).astype(jnp.float32)
    resid_f = rounded(token_rows + attn_rows)
    resid_scale = rms_scale(resid_f)
    ffn_in = lax.all_gather(
        (resid_f * resid_scale).astype(jnp.bfloat16), "tensor", axis=0, tiled=True
    )
    pre_act = jnp.dot(ffn_in, up_full, preferred_element_type=jnp.float32)
    activated = gelu_value(pre_act).astype(jnp.bfloat16)
    ffn_part = jnp.dot(activated, down_full, preferred_element_type=jnp.float32)
    grad_act = contract_last(grad_output, down_full)
    grad_pre = (grad_act * gelu_slope(pre_act)).astype(jnp.bfloat16)
    norm_part = contract_last(grad_pre, up_full)
    ffn_rows_sum = lax.psum_scatter(
        ffn_part.astype(jnp.bfloat16), "tensor", scatter_dimension=0, tiled=True
    ).astype(jnp.float32)
    layer_out = (resid_f + ffn_rows_sum).astype(jnp.bfloat16)
    norm_rows = lax.psum_scatter(
        norm_part.astype(jnp.bfloat16), "tensor", scatter_dimension=0, tiled=True
    ).astype(jnp.float32)
    out_rows = lax.dynamic_slice_in_dim(grad_output, row_start, rows_share, 0).astype(jnp.float32)
    grad_resid_rows = (out_rows + norm_back(resid_f, resid_scale, norm_rows)).astype(jnp.bfloat16)
    grad_resid = lax.all_gather(grad_resid_rows, "tensor", axis=0, tiled=True)
    grad_mix = contract_last(grad_resid, output_weight).astype(jnp.bfloat16)
    mix_heads_grad = grad_mix.reshape(block_count, BLOCK, heads_here, HD)
    grad_probs = jnp.einsum(
        "cqhd,ckhd->chqk", mix_heads_grad, value_heads, preferred_element_type=jnp.float32
    )
    row_dot = jnp.einsum(
        "cqhd,cqhd->chq", mix_heads_grad, head_mix, preferred_element_type=jnp.float32
    )[..., None]
    grad_scores = (attention * (grad_probs - row_dot) * score_factor).astype(jnp.bfloat16)
    grad_query = (
        jnp.einsum("chqk,ckhd->cqhd", grad_scores, key_heads, preferred_element_type=jnp.float32)
        .astype(jnp.bfloat16)
        .reshape(token_count, head_width)
    )
    grad_keys = (
        jnp.einsum("chqk,cqhd->ckhd", grad_scores, query_heads, preferred_element_type=jnp.float32)
        .astype(jnp.bfloat16)
        .reshape(pair_count * NLEN, head_width)
    )
    grad_values = (
        jnp.einsum(
            "chqk,cqhd->ckhd", attention_b, mix_heads_grad, preferred_element_type=jnp.float32
        )
        .astype(jnp.bfloat16)
        .reshape(pair_count * NLEN, head_width)
    )
    summed = lax.psum_scatter(
        jnp.concatenate(
            [
                contract_first(normed, grad_query),
                contract_first(enc_rows, grad_keys),
                contract_first(enc_rows, grad_values),
                contract_first(grad_resid, mix_rows),
            ],
            axis=1,
        ).astype(jnp.bfloat16),
        "dp",
        scatter_dimension=0,
        tiled=True,
    ).astype(jnp.float32)
    query_grad = summed[:, :head_width]
    key_grad = summed[:, head_width : 2 * head_width]
    value_grad = summed[:, 2 * head_width : 3 * head_width]
    mix_grad = summed[:, 3 * head_width :].T
    input_part = contract_last(grad_query, query_weight)
    input_rows = lax.psum_scatter(
        input_part.astype(jnp.bfloat16), "tensor", scatter_dimension=0, tiled=True
    ).astype(jnp.float32)
    grad_tokens = (
        grad_resid_rows.astype(jnp.float32) + norm_back(token_rows, base_rows, input_rows)
    ).astype(jnp.bfloat16)
    return (layer_out, grad_tokens, query_grad, key_grad, value_grad, mix_grad)


def solution(mesh):
    in_specs = (
        P("dp", None),
        P("dp", None, "tensor"),
        P("dp", None),
        P("dp", None),
        P(None, "tensor"),
        P(None, "tensor"),
        P(None, "tensor"),
        P("tensor", None),
        P("dp", "tensor"),
        P("tensor", "dp"),
        P("dp", None),
    )
    out_specs = (
        P(("dp", "tensor"), None),
        P(("dp", "tensor"), None),
        P("dp", "tensor"),
        P("dp", "tensor"),
        P("dp", "tensor"),
        P("tensor", "dp"),
    )
    return jax.shard_map(local, mesh=mesh, in_specs=in_specs, out_specs=out_specs, check_vma=False)
```

profile of v0, /device:TPU:1, one launch (start us, length us, event | category | flops | bytes accessed | tf_op | source)
XLA Modules:
  0.0 749.5 jit_solution(7438209623869843166)
XLA Ops:
  8.0 0.9 copy.48
  9.0 0.8 copy.49
  10.1 16.8 %all_to_all.20 = s32[16,1,2]{2,1,0:T(1,128)S(1)} all-to-all(s32[16,1,2]{2,1,0:T(1,128)S(1)} %copy.50), channel_id=1, replica_groups=mesh['dp'=16,'tensor'=16] {'dp'}, dimensions={0} | all-to-all | bytes 256 | tf_op jit(solution)/shard_map/all_to_all | solution.py:92
  27.2 1.9 gather_fusion
  29.2 1.6 broadcast_select_fusion
  30.7 5.0 all-to-all-start.1
  36.0 48.8 %all-to-all-done.1 = bf16[16,2,128,256]{3,2,1,0:T(8,128)(2,1)} async-done(((bf16[16,2,128,256]{3,2,1,0:T(8,128)(2,1)}), bf16[16,2,128,256]{3,2,1,0:T(8,128)(2,1)}, u32[]{:S(2)}, u32[]{:S(2)}) %all-to-all-start.1) | async-done | bytes 2097184 | tf_op jit(solution)/shard_map/all_to_all | solution.py:89
  84.8 3.0 gather_fusion.1
  87.8 2.0 broadcast_select_fusion.1
  90.3 2.0 convolution_convert_fusion.13
  92.3 78.9 %all-gather.6.cloned.1.call-done = bf16[8,128,4096]{2,1,0:T(8,128)(2,1)} async-done(((bf16[8,128,256]{2,1,0:T(8,128)(2,1)}), bf16[8,128,4096]{2,1,0:T(8,128)(2,1)}) %all-gather.6.cloned.1.call-update) | async-done | bytes 8388624 | tf_op jit(solution)/shard_map/all_gather | solution.py:102
  171.2 6.8 convolution_convert_fusion.10
  178.0 3.0 convolution_convert_fusion.11
  181.1 1.2 fusion.45
  182.3 1.1 convolution_convert_fusion.15
  183.5 2.0 convolution_convert_fusion.1
  186.2 2.5 convert_element_type.123
  188.6 75.0 %reduce-scatter.6.cloned.1.call-done = bf16[16,4096]{1,0:T(8,128)(2,1)} async-done(((bf16[256,4096]{1,0:T(8,128)(2,1)}), bf16[16,4096]{1,0:T(8,128)(2,1)}) %reduce-scatter.6.cloned.1.call-update) | async-done | bytes 131088 | tf_op jit(solution)/shard_map/reduce_scatter | solution.py:142
  263.6 1.0 add_convert_fusion
  266.3 49.1 %all-gather.8.cloned.1.call-done = bf16[256,4096]{1,0:T(8,128)(2,1)} async-done(((bf16[16,4096]{1,0:T(8,128)(2,1)}), bf16[256,4096]{1,0:T(8,128)(2,1)}) %all-gather.8.cloned.1.call-update) | async-done | bytes 2097168 | tf_op jit(solution)/shard_map/all_gather | solution.py:147
  315.4 4.1 fusion.61
  319.5 48.6 %all-gather.12.cloned.1.call-done = bf16[512,4096]{1,0:T(8,128)(2,1)} async-done(((bf16[512,256]{1,0:T(8,128)(2,1)}), bf16[512,4096]{1,0:T(8,128)(2,1)}) %all-gather.12.cloned.1.call-update) | async-done | bytes 4194320 | tf_op jit(solution)/shard_map/all_gather | solution.py:106
  368.1 8.1 %convolution_convert_fusion.2 = bf16[256,4096]{1,0:T(8,128)(2,1)} fusion(bf16[4096,512]{1,0:T(8,128)(2,1)} %all-gather.10.cloned.1.call-done, bf16[256,4096]{1,0:T(8,128)(2,1)} %param.21, bf16[512,4096]{1,0:T(8,128)(2,1)} %all-gather.12.cloned.1.call-done, f32[256,512]{1,0:T(8,128)S(1)} %fusion.61), kind=kOutput, calls=%fused_computation.4 | convolution fusion | flops 2151022592 | bytes 13107200 | tf_op jit(solution)/shard_map/dot_general | solution.py:47
  376.4 4.8 convolution_convert_fusion.3
  381.3 70.9 %reduce-scatter.10.cloned.1.call-done = bf16[16,4096]{1,0:T(8,128)(2,1)} async-done(((bf16[256,4096]{1,0:T(8,128)(2,1)}), bf16[16,4096]{1,0:T(8,128)(2,1)}) %reduce-scatter.10.cloned.1.call-update) | async-done | bytes 131088 | tf_op jit(solution)/shard_map/reduce_scatter | solution.py:160
  452.2 1.1 fusion.31
  453.3 81.3 %reduce-scatter.8.cloned.1.call-done = bf16[16,4096]{1,0:T(8,128)(2,1)} async-done(((bf16[256,4096]{1,0:T(8,128)(2,1)}), bf16[16,4096]{1,0:T(8,128)(2,1)}) %reduce-scatter.8.cloned.1.call-update) | async-done | bytes 131088 | tf_op jit(solution)/shard_map/reduce_scatter | solution.py:156
  534.6 1.8 fusion.26
  536.5 50.2 %all-gather.14.cloned.1.call-done = bf16[256,4096]{1,0:T(8,128)(2,1)} async-done(((bf16[16,4096]{1,0:T(8,128)(2,1)}), bf16[256,4096]{1,0:T(8,128)(2,1)}) %all-gather.14.cloned.1.call-update) | async-done | bytes 2097168 | tf_op jit(solution)/shard_map/all_gather | solution.py:165
  586.7 2.3 convolution_convert_fusion.12
  589.7 1.3 fusion.6
  591.0 1.1 convolution_convert_fusion.14
  592.7 3.3 convolution_convert_fusion
  596.1 1.8 fusion.4
  597.9 1.8 copy.56
  599.7 1.8 fusion.5
  601.6 1.8 copy.57
  603.4 1.5 convolution_convert_fusion.4
  605.7 5.1 convolution_convert_fusion.6
  611.2 1.3 convolution_convert_fusion.5
  612.5 2.3 pad_maximum_fusion
  614.9 59.2 %reduce-scatter.12.cloned.1.call-done = bf16[16,4096]{1,0:T(8,128)(2,1)} async-done(((bf16[256,4096]{1,0:T(8,128)(2,1)}), bf16[16,4096]{1,0:T(8,128)(2,1)}) %reduce-scatter.12.cloned.1.call-update) | async-done | bytes 131088 | tf_op jit(solution)/shard_map/reduce_scatter | solution.py:211
  674.2 1.2 fusion.27
  675.4 1.8 fusion.30
  677.2 60.0 %reduce-scatter.14.cloned.1.call-done = bf16[256,512]{0,1:T(8,128)(2,1)} async-done(((bf16[4096,512]{0,1:T(8,128)(2,1)}), bf16[256,512]{0,1:T(8,128)(2,1)}) %reduce-scatter.14.cloned.1.call-update) | async-done | bytes 262160 | tf_op jit(solution)/shard_map/reduce_scatter | solution.py:192
  737.3 1.0 convert_element_type.162
  738.9 0.9 fusion.60
  739.9 0.8 copy.58
  (87 shorter events, 8.9 us)
Async XLA Ops:
  8.0 175.5 %copy-start = (bf16[128,4096]{1,0:T(8,128)(2,1)S(1)}, bf16[128,4096]{1,0:T(8,128)(2,1)}, u32[]{:S(2)}) copy-start(bf16[128,4096]{1,0:T(8,128)(2,1)} %param.18) | copy-start | bytes 3145732
  29.1 6.6 copy-start.12
  30.7 59.1 %copy-start.2 = (bf16[256,4096]{1,0:T(8,128)(2,1)S(1)}, bf16[256,4096]{1,0:T(8,128)(2,1)}, u32[]{:S(2)}) copy-start(bf16[256,4096]{1,0:T(8,128)(2,1)} %param.11) | copy-start | bytes 6291460
  30.7 54.0 %all-to-all-start.1 = ((bf16[16,2,128,256]{3,2,1,0:T(8,128)(2,1)}), bf16[16,2,128,256]{3,2,1,0:T(8,128)(2,1)}, u32[]{:S(2)}, u32[]{:S(2)}) async-start(bf16[16,2,128,256]{3,2,1,0:T(8,128)(2,1)} %broadcast_select_fusion), calls=%async_computation.1 | async-start | bytes 4194304 | tf_op jit(solution)/shard_map/all_to_all | solution.py:89
  35.7 135.5 %all-gather.6.cloned.1.call-start = ((), (), s32[]{:S(2)}) async-start(), calls=%async_computation.7 | async-start | bytes 8912896 | tf_op jit(solution)/shard_map/all_gather | solution.py:102
  89.8 173.9 %reduce-scatter.6.cloned.1.call-start = ((), (), s32[]{:S(2)}) async-start(), calls=%async_computation.8 | async-start | bytes 2228224 | tf_op jit(solution)/shard_map/reduce_scatter | solution.py:142
  92.3 88.7 %copy-start.11 = (bf16[256,128]{1,0:T(8,128)(2,1)}, bf16[256,128]{1,0:T(8,128)(2,1)S(1)}, u32[]{:S(2)}) copy-start(bf16[256,128]{1,0:T(8,128)(2,1)S(1)} %convolution_convert_fusion.13) | copy-start | bytes 196612
  171.2 6.8 copy-start.13
  171.2 6.8 copy-start.14
  183.4 405.6 %copy-start.5 = (bf16[4,128,64]{1,2,0:T(8,128)(2,1)}, bf16[4,128,64]{1,2,0:T(8,128)(2,1)S(1)}, u32[]{:S(2)}) copy-start(bf16[4,128,64]{1,2,0:T(8,128)(2,1)S(1)} %convolution_convert_fusion.15) | copy-start | bytes 196612
  185.5 80.8 %all-gather.10.cloned.1.call-start = ((), (), s32[]{:S(2)}) async-start(), calls=%async_computation.10 | async-start | bytes 4456448 | tf_op jit(solution)/shard_map/all_gather | solution.py:105
  186.1 129.3 %all-gather.8.cloned.1.call-start = ((), (), s32[]{:S(2)}) async-start(), calls=%async_computation.9 | async-start | bytes 2228224 | tf_op jit(solution)/shard_map/all_gather | solution.py:147
  265.6 102.5 %all-gather.12.cloned.1.call-start = ((), (), s32[]{:S(2)}) async-start(), calls=%async_computation.11 | async-start | bytes 4456448 | tf_op jit(solution)/shard_map/all_gather | solution.py:106
  266.2 186.0 %reduce-scatter.10.cloned.1.call-start = ((), (), s32[]{:S(2)}) async-start(), calls=%async_computation.13 | async-start | bytes 2228224 | tf_op jit(solution)/shard_map/reduce_scatter | solution.py:160
  376.2 158.4 %reduce-scatter.8.cloned.1.call-start = ((), (), s32[]{:S(2)}) async-start(), calls=%async_computation.12 | async-start | bytes 2228224 | tf_op jit(solution)/shard_map/reduce_scatter | solution.py:156
  381.3 205.5 %all-gather.14.cloned.1.call-start = ((), (), s32[]{:S(2)}) async-start(), calls=%async_computation.14 | async-start | bytes 2228224 | tf_op jit(solution)/shard_map/all_gather | solution.py:165
  536.4 137.7 %reduce-scatter.12.cloned.1.call-start = ((), (), s32[]{:S(2)}) async-start(), calls=%async_computation.15 | async-start | bytes 2228224 | tf_op jit(solution)/shard_map/reduce_scatter | solution.py:211
  589.0 0.6 copy-start.6
  589.7 13.7 %copy-start.1 = (bf16[256,4096]{1,0:T(8,128)(2,1)S(1)}, bf16[256,4096]{1,0:T(8,128)(2,1)}, u32[]{:S(2)}) copy-start(bf16[256,4096]{1,0:T(8,128)(2,1)} %all-gather.14.cloned.1.call-done) | copy-start | bytes 6291460
  592.1 0.6 copy-start.7
  596.0 141.2 %reduce-scatter.14.cloned.1.call-start = ((), (), s32[]{:S(2)}) async-start(), calls=%async_computation.16 | async-start | bytes 4456448 | tf_op jit(solution)/shard_map/reduce_scatter | solution.py:192
  597.9 6.9 copy-start.8
  603.4 1.6 copy-start.3
  603.4 2.3 copy-start.9
  605.0 5.8 slice-start
  605.6 5.2 copy-start.10
  605.7 5.5 slice-start.1
  614.8 60.6 %copy-start.4 = (bf16[16,4096]{1,0:T(8,128)(2,1)S(1)}, bf16[16,4096]{1,0:T(8,128)(2,1)}, u32[]{:S(2)}) copy-start(bf16[16,4096]{1,0:T(8,128)(2,1)} %get-tuple-element.33) | copy-start | bytes 393220
Sparse Core Ops, SparseCore 0:
  89.9 81.2 all-gather.5
  185.6 77.9 reduce-scatter.5
  536.6 50.1 all-gather.13
  596.1 77.9 reduce-scatter.11
  676.6 60.6 reduce-scatter.13
Sparse Core Ops, SparseCore 1:
  187.8 43.1 all-gather.9
  265.7 49.7 all-gather.7
  317.2 50.9 all-gather.11
  376.3 75.9 reduce-scatter.9
  455.8 78.8 reduce-scatter.7
where the time goes:
time: 753 us; the launch traced here: 749 us
  waiting for transfers between devices  623 us (83%)
  matrix products  53.3 us (7%)
  other arithmetic  18.1 us (2%)
  blocking collectives  16.8 us (2%)
  local copies, waits for them, and re-layouts  16.6 us (2%)
  between operations  15.8 us (2%)
    reduce_scatter x1, waiting for transfers between devices, local(): lax.psum_scatter(ffn_part.astype(jnp.bfloat16), 'tensor', scatter_dimensi...  81.3 us
    all_gather x1, waiting for transfers between devices, local(): encodings = lax.all_gather(local_enc, 'tensor', axis=2, tiled=True)  78.9 us
    reduce_scatter x1, waiting for transfers between devices, local(): lax.psum_scatter(attn_part.astype(jnp.bfloat16), 'tensor', scatter_dimens...  75 us
    reduce_scatter x1, waiting for transfers between devices, local(): lax.psum_scatter(norm_part.astype(jnp.bfloat16), 'tensor', scatter_dimens...  70.9 us
    reduce_scatter x1, waiting for transfers between devices, local(): lax.psum_scatter(jnp.concatenate([contract_first(normed, grad_query), con...  60 us
    reduce_scatter x1, waiting for transfers between devices, local(): lax.psum_scatter(input_part.astype(jnp.bfloat16), 'tensor', scatter_dimen...  59.2 us
    all_gather x1, waiting for transfers between devices, local(): grad_resid = lax.all_gather(grad_resid_rows, 'tensor', axis=0, tiled=True)  50.2 us
    all_gather x1, waiting for transfers between devices, local(): lax.all_gather((resid_f * resid_scale).astype(jnp.bfloat16), 'tensor', ax...  49.1 us
  transfers between devices with their start and end apart: 11, of which 10 were waited for; matrix products, arithmetic and copies ran while one was open for 5% of the time, Pallas kernels for 0%

commit v1 on v0

v1 whole, which is shorter than its diff:
```python
import math

import jax
import jax.numpy as jnp
from jax import lax
from jax.sharding import PartitionSpec as P

HD = 128
BLOCK = 64
NLEN = 128
SIDE = 4
DATA = ("z", "core")
PLANE = ("y", "x")


epsilon = 1e-06
gelu_root = 0.7978845608028654
gelu_cubic = 0.044715


def rms_scale(values):
    return lax.rsqrt(jnp.mean(values * values, axis=-1, keepdims=True) + epsilon)


def norm_back(values, factor, incoming):
    normal_part = values * factor
    return (
        incoming - normal_part * jnp.mean(incoming * normal_part, axis=-1, keepdims=True)
    ) * factor


def gelu_value(inputs):
    inner = gelu_root * (inputs + gelu_cubic * inputs * inputs * inputs)
    return 0.5 * inputs * (1.0 + jnp.tanh(inner))


def gelu_slope(inputs):
    inner = gelu_root * (inputs + gelu_cubic * inputs * inputs * inputs)
    tanh_part = jnp.tanh(inner)
    return 0.5 * (1.0 + tanh_part) + 0.5 * inputs * (1.0 - tanh_part * tanh_part) * gelu_root * (
        1.0 + 3.0 * gelu_cubic * inputs * inputs
    )


def rounded(partial_value):
    return lax.optimization_barrier(partial_value.astype(jnp.bfloat16)).astype(jnp.float32)


def contract_last(left_side, right_side):
    return lax.dot_general(
        left_side, right_side, (((1,), (1,)), ((), ())), preferred_element_type=jnp.float32
    )


def contract_first(left_side, right_side):
    return lax.dot_general(
        left_side, right_side, (((0,), (0,)), ((), ())), preferred_element_type=jnp.float32
    )


def copies_to(rows, axis):
    size = lax.axis_size(axis)
    copies = jnp.broadcast_to(rows[None], (size,) + rows.shape)
    gathered = lax.all_to_all(copies, axis, split_axis=0, concat_axis=0, tiled=True)
    return gathered.reshape(size * rows.shape[0], rows.shape[1])


def scatter_sum(partial_rows, axis):
    size = lax.axis_size(axis)
    share = partial_rows.shape[0] // size
    swapped = lax.all_to_all(
        partial_rows.astype(jnp.bfloat16).reshape(size, share, partial_rows.shape[1]),
        axis,
        split_axis=0,
        concat_axis=0,
        tiled=True,
    )
    return jnp.sum(swapped.astype(jnp.float32), axis=0)


def heads_of_block(own_head_blocks):
    here = lax.axis_index("y")
    heads = lax.dynamic_update_index_in_dim(
        jnp.zeros_like(own_head_blocks),
        lax.dynamic_index_in_dim(own_head_blocks, here, 0, keepdims=False),
        here,
        0,
    )
    for step in range(1, SIDE):
        sent = lax.dynamic_index_in_dim(
            own_head_blocks, lax.rem(here + step, SIDE), 0, keepdims=False
        )
        got = lax.ppermute(
            sent, "y", [(place, (place + step) % SIDE) for place in range(SIDE)]
        )
        heads = lax.dynamic_update_index_in_dim(heads, got, lax.rem(here + SIDE - step, SIDE), 0)
    return heads


def data_sum(partial_rows, after):
    core = lax.axis_index("core")
    shares = partial_rows.reshape(lax.axis_size("z"), 2, -1, partial_rows.shape[1])
    given = lax.dynamic_index_in_dim(shares, 1 - core, 1, keepdims=False)
    kept = lax.dynamic_index_in_dim(shares, core, 1, keepdims=False)
    got = lax.ppermute(given, "core", [(0, 1), (1, 0)])
    paired = (kept.astype(jnp.float32) + got.astype(jnp.float32)).astype(jnp.bfloat16)
    paired, after = lax.optimization_barrier((paired, after))
    summed = lax.psum_scatter(
        paired.reshape(-1, paired.shape[2]), "z", scatter_dimension=0, tiled=True
    )
    return summed, after


def local(
    tokens,
    neighbour_buffer,
    shard_ids,
    row_ids,
    query_weight,
    key_weight,
    value_weight,
    output_weight,
    up_weight,
    down_weight,
    grad_output,
):
    data_size = lax.axis_size(DATA)
    tensor_size = lax.axis_size(PLANE)
    token_count = tokens.shape[0]
    width = tokens.shape[1]
    block_count = shard_ids.shape[0]
    capacity = block_count // 2
    pair_count = 2 * block_count
    owners = shard_ids.reshape(pair_count)
    wanted = row_ids.reshape(pair_count)
    same_owner = owners[:, None] == owners[None, :]
    earlier = lax.broadcasted_iota(jnp.int32, (pair_count, pair_count), 0) < lax.broadcasted_iota(
        jnp.int32, (pair_count, pair_count), 1
    )
    slot_index = jnp.sum((same_owner & earlier).astype(jnp.int32), axis=0)
    owner_grid = lax.broadcasted_iota(jnp.int32, (data_size, capacity, pair_count), 0)
    slot_grid = lax.broadcasted_iota(jnp.int32, (data_size, capacity, pair_count), 1)
    slot_match = (owners[None, None, :] == owner_grid) & (slot_index[None, None, :] == slot_grid)
    requests = jnp.sum(jnp.where(slot_match, wanted[None, None, :], 0), axis=2)
    asked = lax.all_to_all(requests, DATA, split_axis=0, concat_axis=0, tiled=True)
    replies = lax.all_to_all(
        jnp.take(neighbour_buffer, asked, axis=0, mode="clip"),
        DATA,
        split_axis=0,
        concat_axis=0,
        tiled=True,
    )
    reply_rows = replies.reshape((data_size * capacity,) + replies.shape[2:])
    mine = jnp.take(reply_rows, owners * capacity + slot_index, axis=0, mode="clip")
    enc_mine = mine.reshape(pair_count * NLEN, -1).T
    both_weights = lax.all_gather(
        jnp.concatenate([key_weight, value_weight], axis=1), "y", axis=0, tiled=False
    )
    output_heads = lax.all_gather(output_weight, "y", axis=0, tiled=True)
    token_f = tokens.astype(jnp.float32)
    base_scale = rms_scale(token_f)
    normed = (token_f * base_scale).astype(jnp.bfloat16)
    query_rows = jnp.dot(normed, query_weight, preferred_element_type=jnp.float32).astype(
        jnp.bfloat16
    )
    query_heads = heads_of_block(query_rows.reshape(block_count, BLOCK, HD))
    enc_mine, both_weights, query_heads = lax.optimization_barrier(
        (enc_mine, both_weights, query_heads)
    )
    features, enc_columns = enc_mine.shape
    keys_here = 2 * NLEN
    block_pieces = jnp.swapaxes(enc_mine.reshape(features, SIDE, keys_here), 0, 1)
    enc_block = lax.all_to_all(
        jnp.broadcast_to(
            block_pieces[:, None], (SIDE, SIDE, features, keys_here)
        ).reshape(SIDE * SIDE, features, keys_here),
        PLANE,
        split_axis=0,
        concat_axis=0,
        tiled=True,
    ).reshape(width, keys_here)
    frozen = jnp.concatenate([up_weight, down_weight.T], axis=1)
    enc_block, output_heads, frozen = lax.optimization_barrier((enc_block, output_heads, frozen))
    frozen_full = lax.all_gather(frozen, DATA, axis=0, tiled=True)
    hidden = up_weight.shape[1]
    up_full = frozen_full[:, :hidden]
    down_turned = frozen_full[:, hidden:]
    both_heads = jnp.stack(
        [
            contract_first(enc_block, both_weights[head]).astype(jnp.bfloat16)
            for head in range(SIDE)
        ]
    )
    key_heads = both_heads[:, :, :HD]
    value_heads = both_heads[:, :, HD:]
    score_factor = 1.0 / math.sqrt(HD)
    scores = (
        jnp.einsum("hqd,hkd->hqk", query_heads, key_heads, preferred_element_type=jnp.float32)
        * score_factor
    )
    raised = jnp.exp(scores)
    attention = raised / jnp.sum(raised, axis=-1, keepdims=True)
    attention_b = attention.astype(jnp.bfloat16)
    head_mix = jnp.einsum(
        "hqk,hkd->hqd", attention_b, value_heads, preferred_element_type=jnp.float32
    ).astype(jnp.bfloat16)
    mix_rows = jnp.swapaxes(head_mix, 0, 1).reshape(BLOCK, SIDE * HD)
    attn_part = jnp.dot(mix_rows, output_heads, preferred_element_type=jnp.float32)
    rows_share = token_count // tensor_size
    row_start = lax.axis_index(PLANE) * rows_share
    token_rows = lax.dynamic_slice_in_dim(tokens, row_start, rows_share, 0).astype(jnp.float32)
    base_rows = lax.dynamic_slice_in_dim(base_scale, row_start, rows_share, 0)
    attn_rows, enc_mine = lax.optimization_barrier((scatter_sum(attn_part, "x"), enc_mine))
    enc_full = lax.all_gather(enc_mine, PLANE, axis=0, tiled=True)
    resid_f = rounded(token_rows + attn_rows)
    resid_scale = rms_scale(resid_f)
    ffn_in = copies_to((resid_f * resid_scale).astype(jnp.bfloat16), PLANE)
    grad_act = lax.optimization_barrier(
        jnp.dot(grad_output, down_turned, preferred_element_type=jnp.float32)
    )
    pre_act = jnp.dot(ffn_in, up_full, preferred_element_type=jnp.float32)
    activated = gelu_value(pre_act).astype(jnp.bfloat16)
    grad_pre = (grad_act * gelu_slope(pre_act)).astype(jnp.bfloat16)
    norm_part = contract_last(grad_pre, up_full)
    ffn_part = contract_last(activated, down_turned).astype(jnp.bfloat16)
    norm_rows = scatter_sum(norm_part, PLANE)
    out_rows = lax.dynamic_slice_in_dim(grad_output, row_start, rows_share, 0).astype(jnp.float32)
    grad_resid_rows = (out_rows + norm_back(resid_f, resid_scale, norm_rows)).astype(jnp.bfloat16)
    grad_block = copies_to(grad_resid_rows, "x")
    grad_resid = lax.all_gather(grad_block, "y", axis=0, tiled=True)
    grad_mix = contract_last(grad_block, output_heads).astype(jnp.bfloat16)
    mix_heads_grad = jnp.swapaxes(grad_mix.reshape(BLOCK, SIDE, HD), 0, 1)
    grad_probs = jnp.einsum(
        "hqd,hkd->hqk", mix_heads_grad, value_heads, preferred_element_type=jnp.float32
    )
    row_dot = jnp.einsum(
        "hqd,hqd->hq", mix_heads_grad, head_mix, preferred_element_type=jnp.float32
    )[..., None]
    grad_scores = (attention * (grad_probs - row_dot) * score_factor).astype(jnp.bfloat16)
    grad_query = jnp.einsum(
        "hqk,hkd->hqd", grad_scores, key_heads, preferred_element_type=jnp.float32
    ).astype(jnp.bfloat16)
    grad_keys = jnp.einsum(
        "hqk,hqd->hkd", grad_scores, query_heads, preferred_element_type=jnp.float32
    ).astype(jnp.bfloat16)
    grad_values = jnp.einsum(
        "hqk,hqd->hkd", attention_b, mix_heads_grad, preferred_element_type=jnp.float32
    ).astype(jnp.bfloat16)
    swapped = lax.all_to_all(
        jnp.concatenate([grad_keys, grad_values, grad_query, head_mix], axis=1),
        "y",
        split_axis=0,
        concat_axis=0,
        tiled=True,
    )
    swapped, ffn_part = lax.optimization_barrier((swapped, ffn_part))
    both_grads = jnp.concatenate(
        [
            swapped[:, :keys_here].reshape(enc_columns, HD),
            swapped[:, keys_here : 2 * keys_here].reshape(enc_columns, HD),
        ],
        axis=1,
    )
    query_grads = swapped[:, 2 * keys_here : 2 * keys_here + BLOCK].reshape(token_count, HD)
    mix_back = swapped[:, 2 * keys_here + BLOCK :].reshape(token_count, HD)
    weight_parts = jnp.concatenate(
        [
            contract_first(normed, query_grads),
            jnp.dot(enc_full, both_grads, preferred_element_type=jnp.float32),
            contract_first(grad_resid, mix_back),
        ],
        axis=1,
    ).astype(jnp.bfloat16)
    summed, query_grads = data_sum(weight_parts, query_grads)
    summed = summed.astype(jnp.float32)
    query_grad = summed[:, :HD]
    key_grad = summed[:, HD : 2 * HD]
    value_grad = summed[:, 2 * HD : 3 * HD]
    mix_grad = summed[:, 3 * HD :].T
    layer_out = (resid_f + scatter_sum(ffn_part, PLANE)).astype(jnp.bfloat16)
    input_part = contract_last(query_grads, query_weight)
    input_rows = scatter_sum(input_part, PLANE)
    grad_tokens = (
        grad_resid_rows.astype(jnp.float32) + norm_back(token_rows, base_rows, input_rows)
    ).astype(jnp.bfloat16)
    return (layer_out, grad_tokens, query_grad, key_grad, value_grad, mix_grad)


def solution(mesh):
    mesh = jax.sharding.Mesh(
        mesh.devices.reshape(-1, 2, SIDE, SIDE), DATA + PLANE
    )
    in_specs = (
        P(DATA, None),
        P(DATA, None, PLANE),
        P(DATA, None),
        P(DATA, None),
        P(None, PLANE),
        P(None, PLANE),
        P(None, PLANE),
        P(PLANE, None),
        P(DATA, PLANE),
        P(PLANE, DATA),
        P(DATA, None),
    )
    out_specs = (
        P(DATA + PLANE, None),
        P(DATA + PLANE, None),
        P(DATA, PLANE),
        P(DATA, PLANE),
        P(DATA, PLANE),
        P(PLANE, DATA),
    )
    return jax.shard_map(local, mesh=mesh, in_specs=in_specs, out_specs=out_specs, check_vma=False)
```

time: 753 us -> 485 us (0.64)
  waiting for transfers between devices: 623 us -> 231 us
  blocking collectives: 16.8 us -> 67.9 us
  starting transfers between devices: 5.55 us -> 40.1 us
  local copies, waits for them, and re-layouts: 16.6 us -> 42.3 us
  other arithmetic: 18.1 us -> 27.4 us
    reduce_scatter x5 -> x1, waiting for transfers between devices: 346 us -> 0.01 us  [data_sum(): lax.psum_scatter(paired.reshape(-1, paired.shape[2]), 'z', scatter_dimens...]
    all_gather x5, waiting for transfers between devices: 227 us -> 120 us  [the longest x1 57.5 us: local(): output_heads = lax.all_gather(output_weight, 'y', axis=0, tiled=True)]
    all_to_all x1 -> x7, waiting for transfers between devices: 48.8 us -> 108 us  [the longest x2 50.5 us: scatter_sum(): lax.all_to_all(partial_rows.astype(jnp.bfloat16).reshape(size, share, par...]
    all_to_all x1 -> x3, blocking collectives: 16.8 us -> 67.9 us  [the longest x2 51.1 us: scatter_sum(): lax.all_to_all(partial_rows.astype(jnp.bfloat16).reshape(size, share, par...]
    all_to_all x1 -> x7, starting transfers between devices: 4.95 us -> 34.2 us  [the longest x2 9.75 us: scatter_sum(): lax.all_to_all(partial_rows.astype(jnp.bfloat16).reshape(size, share, par...]
    dot_general x4 -> x6, matrix products: 8.55 us -> 18.7 us  [contract_first(): lax.dot_general(left_side, right_side, (((0,), (0,)), ((), ())), preferre...]
    dot_general x0 -> x2, local copies, waits for them, and re-layouts: none -> 8.18 us  [contract_first(): lax.dot_general(left_side, right_side, (((0,), (0,)), ((), ())), preferre...]
  transfers between devices with their start and end apart: 11 -> 17, of which waited for: 10 -> 11; matrix products, arithmetic and copies ran while one was open for 5% -> 22% of each run, Pallas kernels for 0% -> 0%
where the time goes in v1:
time: 485 us; the launch traced here: 483 us
  waiting for transfers between devices  231 us (48%)
  blocking collectives  67.9 us (14%)
  matrix products  60.2 us (12%)
  local copies, waits for them, and re-layouts  42.3 us (9%)
  starting transfers between devices  40.1 us (8%)
  other arithmetic  27.4 us (6%)
  between operations  14.5 us (3%)
    all_gather x1, waiting for transfers between devices, local(): output_heads = lax.all_gather(output_weight, 'y', axis=0, tiled=True)  57.5 us
    all_to_all x2, blocking collectives, scatter_sum(): lax.all_to_all(partial_rows.astype(jnp.bfloat16).reshape(size, share, par...  51.1 us
    all_to_all x2, waiting for transfers between devices, scatter_sum(): lax.all_to_all(partial_rows.astype(jnp.bfloat16).reshape(size, share, par...  50.5 us
    all_to_all x1, waiting for transfers between devices, local(): lax.all_to_all(jnp.take(neighbour_buffer, asked, axis=0, mode='clip'), DA...  40.6 us
    all_gather x1, waiting for transfers between devices, local(): frozen_full = lax.all_gather(frozen, DATA, axis=0, tiled=True)  30.1 us
    all_gather x1, waiting for transfers between devices, local(): grad_resid = lax.all_gather(grad_block, 'y', axis=0, tiled=True)  20.9 us
    dot_general x6, matrix products, contract_first(): lax.dot_general(left_side, right_side, (((0,), (0,)), ((), ())), preferre...  18.7 us
    all_to_all x1, blocking collectives, local(): lax.all_to_all(requests, DATA, split_axis=0, concat_axis=0, tiled=True)  16.8 us
  transfers between devices with their start and end apart: 17, of which 11 were waited for; matrix products, arithmetic and copies ran while one was open for 22% of the time, Pallas kernels for 0%

profile of v1, /device:TPU:1, one launch (start us, length us, event | category | flops | bytes accessed | tf_op | source)
XLA Modules:
  0.0 483.3 jit_solution(9797347933810615396)
XLA Ops:
  7.2 3.2 pad_maximum_fusion.1
  11.9 16.8 %all_to_all.54 = s32[16,1,2]{2,1,0:T(1,128)S(1)} all-to-all(s32[16,1,2]{2,1,0:T(1,128)S(1)} %copy.79), channel_id=1, replica_groups=mesh['z'=8,'core'=2,'y'=4,'x'=4] {'z','core'}, dimensions={0} | all-to-all | bytes 256 | tf_op jit(solution)/shard_map/all_to_all | solution.py:145
  29.9 2.0 gather_fusion
  32.0 5.1 %all-to-all-start.1 = ((bf16[16,2,128,256]{3,2,1,0:T(8,128)(2,1)}), bf16[16,2,128,256]{3,2,1,0:T(8,128)(2,1)}, u32[]{:S(2)}, u32[]{:S(2)}) async-start(bf16[16,2,128,256]{3,2,1,0:T(8,128)(2,1)} %bitcast.147), calls=%async_computation.1 | async-start | bytes 4194304 | tf_op jit(solution)/shard_map/all_to_all | solution.py:146
  39.6 2.6 collective-permute-start.1
  45.6 40.6 %all-to-all-done.1 = bf16[16,2,128,256]{3,2,1,0:T(8,128)(2,1)} async-done(((bf16[16,2,128,256]{3,2,1,0:T(8,128)(2,1)}), bf16[16,2,128,256]{3,2,1,0:T(8,128)(2,1)}, u32[]{:S(2)}, u32[]{:S(2)}) %all-to-all-start.1) | async-done | bytes 2097184 | tf_op jit(solution)/shard_map/all_to_all | solution.py:146
  86.1 3.0 gather_fusion.1
  89.1 11.7 %all-gather.15.cloned.1.call-done = bf16[16384,256]{1,0:T(8,128)(2,1)} async-done(((bf16[4096,256]{1,0:T(8,128)(2,1)}), bf16[16384,256]{1,0:T(8,128)(2,1)}) %all-gather.15.cloned.1.call-update) | async-done | bytes 8388624 | tf_op jit(solution)/shard_map/all_gather | solution.py:156
  100.8 2.0 copy.81
  102.9 2.6 broadcast_in_dim.67
  105.5 6.3 %all-to-all-start.2 = ((bf16[16,256,256]{2,1,0:T(8,128)(2,1)}), bf16[16,256,256]{2,1,0:T(8,128)(2,1)}, u32[]{:S(2)}, u32[]{:S(2)}) async-start(bf16[16,256,256]{2,1,0:T(8,128)(2,1)} %bitcast.146), calls=%async_computation.2 | async-start | bytes 4194304 | tf_op jit(solution)/shard_map/all_to_all | solution.py:173
  114.7 57.5 %all-gather.7.cloned.1.call-done = bf16[512,4096]{1,0:T(8,128)(2,1)} async-done(((bf16[128,4096]{1,0:T(8,128)(2,1)}), bf16[512,4096]{1,0:T(8,128)(2,1)}) %all-gather.7.cloned.1.call-update) | async-done | bytes 4194320 | tf_op jit(solution)/shard_map/all_gather | solution.py:159
  172.3 3.0 fusion.40
  175.3 3.0 fusion.43
  178.3 3.0 fusion.46
  181.3 3.0 fusion.49
  187.4 3.1 convolution_convert_fusion.4
  190.5 12.3 %all_to_all.55 = bf16[4,16,4096]{2,1,0:T(8,128)(2,1)S(1)} all-to-all(bf16[4,16,4096]{2,1,0:T(8,128)(2,1)S(1)} %bitcast.153), channel_id=1, replica_groups=mesh['z'=8,'core'=2,'y'=4,'x'=4] {'x'}, dimensions={0} | all-to-all | bytes 1048576 | tf_op jit(solution)/shard_map/all_to_all | solution.py:71
  204.8 4.6 all-to-all-start.4
  209.4 30.1 %all-gather.9.cloned.1.call-done = bf16[4096,1024]{0,1:T(8,128)(2,1)} async-done(((bf16[256,1024]{0,1:T(8,128)(2,1)}), bf16[4096,1024]{0,1:T(8,128)(2,1)}) %all-gather.9.cloned.1.call-update) | async-done | bytes 8388624 | tf_op jit(solution)/shard_map/all_gather | solution.py:184
  239.5 5.0 %fusion.21 = f32[256,512]{0,1:T(8,128)} fusion(bf16[256,4096]{1,0:T(8,128)(2,1)} %param.21, bf16[4096,1024]{0,1:T(8,128)(2,1)} %all-gather.9.cloned.1.call-done), kind=kOutput, calls=%fused_computation.39 | convolution fusion | flops 1073741824 | bytes 6815744 | tf_op jit(solution)/shard_map/dot_general | solution.py:219
  244.5 4.3 fusion.4
  251.3 38.8 %all_to_all.56 = bf16[16,16,4096]{2,1,0:T(8,128)(2,1)S(1)} all-to-all(bf16[16,16,4096]{2,1,0:T(8,128)(2,1)S(1)} %bitcast.156), channel_id=1, replica_groups=mesh['z'=8,'core'=2,'y'=4,'x'=4] {'y','x'}, dimensions={0} | all-to-all | bytes 4194304 | tf_op jit(solution)/shard_map/all_to_all | solution.py:71
  292.5 4.1 all-to-all-start.6
  298.6 12.0 %all-to-all-done.6 = bf16[4,16,4096]{2,1,0:T(8,128)(2,1)} async-done(((bf16[4,16,4096]{2,1,0:T(8,128)(2,1)}), bf16[4,16,4096]{2,1,0:T(8,128)(2,1)}, u32[]{:S(2)}, u32[]{:S(2)}) %all-to-all-start.6) | async-done | bytes 524320 | tf_op jit(solution)/shard_map/all_to_all | solution.py:64
  310.6 3.8 fusion.52
  314.5 2.2 convolution_convert_fusion.7
  322.9 4.4 all-to-all-start.7
  327.3 1.9 fusion.53
  329.2 4.1 copy.110
  333.3 5.1 %convolution_convert_fusion.2 = bf16[256,4096]{1,0:T(8,128)(2,1)} fusion(bf16[4096,1024]{0,1:T(8,128)(2,1)} %all-gather.9.cloned.1.call-done, f32[256,512]{0,1:T(8,128)} %copy-done.11), kind=kOutput, calls=%fused_computation.6 | convolution fusion | flops 1075970048 | bytes 6815744 | tf_op jit(solution)/shard_map/dot_general | solution.py:50
  338.4 4.7 all-to-all-done.7
  344.0 3.4 convolution_convert_fusion.6
  347.4 2.3 copy.96
  351.6 7.3 %convolution_convert_fusion.1 = bf16[4096,256]{1,0:T(8,128)(2,1)} fusion(bf16[4096,1024]{0,1:T(8,128)(2,1)} %all-gather.11.cloned.1.call-done, bf16[1024,128]{1,0:T(8,128)(2,1)} %bitcast.163, bf16[1024,128]{1,0:T(8,128)(2,1)} %bitcast.162), kind=kOutput, calls=%fused_computation.5 | convolution fusion | flops 2149580800 | bytes 11010048 | tf_op jit(solution)/shard_map/dot_general | solution.py:269
  358.9 20.9 %all-gather.13.cloned.1.call-done = bf16[256,4096]{1,0:T(8,128)(2,1)} async-done(((bf16[64,4096]{1,0:T(8,128)(2,1)}), bf16[256,4096]{1,0:T(8,128)(2,1)}) %all-gather.13.cloned.1.call-update) | async-done | bytes 2097168 | tf_op jit(solution)/shard_map/all_gather | solution.py:230
  379.9 4.1 copy.94
  384.0 3.4 convolution_convert_fusion.5
  387.4 2.3 copy.97
  389.6 2.4 pad_maximum_fusion
  395.3 5.3 %all-to-all-start.8 = ((bf16[16,16,4096]{2,1,0:T(8,128)(2,1)}), bf16[16,16,4096]{2,1,0:T(8,128)(2,1)}, u32[]{:S(2)}, u32[]{:S(2)}) async-start(bf16[16,16,4096]{2,1,0:T(8,128)(2,1)} %bitcast.154), calls=%async_computation.8 | async-start | bytes 4194304 | tf_op jit(solution)/shard_map/all_to_all | solution.py:71
  400.7 4.2 fusion.2
  404.9 4.0 copy.113
  409.0 2.0 convolution_convert_fusion
  411.0 23.1 %all-to-all-done.8 = bf16[16,16,4096]{2,1,0:T(8,128)(2,1)} async-done(((bf16[16,16,4096]{2,1,0:T(8,128)(2,1)}), bf16[16,16,4096]{2,1,0:T(8,128)(2,1)}, u32[]{:S(2)}, u32[]{:S(2)}) %all-to-all-start.8) | async-done | bytes 2097184 | tf_op jit(solution)/shard_map/all_to_all | solution.py:71
  434.1 4.4 all-to-all-start.9
  438.6 1.9 convert_reduce_fusion.1
  441.3 27.4 %all-to-all-done.9 = bf16[16,16,4096]{2,1,0:T(8,128)(2,1)} async-done(((bf16[16,16,4096]{2,1,0:T(8,128)(2,1)}), bf16[16,16,4096]{2,1,0:T(8,128)(2,1)}, u32[]{:S(2)}, u32[]{:S(2)}) %all-to-all-start.9) | async-done | bytes 2097184 | tf_op jit(solution)/shard_map/all_to_all | solution.py:71
  (111 shorter events, 44.4 us)
Async XLA Ops:
  7.2 30.4 %copy-start = (bf16[4096,128]{1,0:T(8,128)(2,1)S(1)}, bf16[4096,128]{1,0:T(8,128)(2,1)}, u32[]{:S(2)}) copy-start(bf16[4096,128]{1,0:T(8,128)(2,1)} %param.15) | copy-start | bytes 3145732
  7.2 93.6 %all-gather.15.cloned.1.call-start = ((), (), s32[]{:S(2)}) async-start(), calls=%async_computation.16 | async-start | bytes 10485760 | tf_op jit(solution)/shard_map/all_gather | solution.py:156
  10.4 0.8 copy-start.9
  10.4 1.0 copy-start.8
  10.4 19.5 %copy-start.3 = (bf16[16,128,256]{2,1,0:T(8,128)(2,1)S(1)}, bf16[16,128,256]{2,1,0:T(8,128)(2,1)}, u32[]{:S(2)}) copy-start(bf16[16,128,256]{2,1,0:T(8,128)(2,1)} %param.12) | copy-start | bytes 3145732
  10.5 161.8 %all-gather.7.cloned.1.call-start = ((), (), s32[]{:S(2)}) async-start(), calls=%async_computation.11 | async-start | bytes 5242880 | tf_op jit(solution)/shard_map/all_gather | solution.py:159
  32.0 5.1 %copy-start.2 = (bf16[256,4096]{1,0:T(8,128)(2,1)S(1)}, bf16[256,4096]{1,0:T(8,128)(2,1)}, u32[]{:S(2)}) copy-start(bf16[256,4096]{1,0:T(8,128)(2,1)} %param.11) | copy-start | bytes 6291460
  32.0 54.2 %all-to-all-start.1 = ((bf16[16,2,128,256]{3,2,1,0:T(8,128)(2,1)}), bf16[16,2,128,256]{3,2,1,0:T(8,128)(2,1)}, u32[]{:S(2)}, u32[]{:S(2)}) async-start(bf16[16,2,128,256]{3,2,1,0:T(8,128)(2,1)} %bitcast.147), calls=%async_computation.1 | async-start | bytes 4194304 | tf_op jit(solution)/shard_map/all_to_all | solution.py:146
  38.4 5.1 %collective-permute-start = (bf16[64,128]{1,0:T(8,128)(2,1)S(1)}, bf16[64,128]{1,0:T(8,128)(2,1)S(1)}, u32[]{:S(2)}, u32[]{:S(2)}) collective-permute-start(bf16[64,128]{1,0:T(8,128)(2,1)S(1)} %get-tuple-element.63), channel_id=1, source_target_pairs={{0,4},{4,8},{8,12},{12,0},{1,5},{5,9},{9,13},{13,1},{2,6},{6,10},{... | collective-permute-start | bytes 49160 | tf_op jit(solution)/shard_map/ppermute | solution.py:93
  39.6 5.1 %collective-permute-start.1 = (bf16[64,128]{1,0:T(8,128)(2,1)S(1)}, bf16[64,128]{1,0:T(8,128)(2,1)S(1)}, u32[]{:S(2)}, u32[]{:S(2)}) collective-permute-start(bf16[64,128]{1,0:T(8,128)(2,1)S(1)} %get-tuple-element.62), channel_id=1, source_target_pairs={{0,8},{4,12},{8,0},{12,4},{1,9},{5,13},{9,1},{13,5},{2,10},{6,14},... | collective-permute-start | bytes 49160 | tf_op jit(solution)/shard_map/ppermute | solution.py:93
  42.2 3.3 collective-permute-start.2
  45.6 138.8 %copy-start.7 = (bf16[4,64,128]{2,1,0:T(8,128)(2,1)}, bf16[4,64,128]{2,1,0:T(8,128)(2,1)S(1)}, u32[]{:S(2)}) copy-start(bf16[4,64,128]{2,1,0:T(8,128)(2,1)S(1)} %bitcast_dynamic-update-slice_fusion) | copy-start | bytes 196612
  105.5 66.8 %all-to-all-start.2 = ((bf16[16,256,256]{2,1,0:T(8,128)(2,1)}), bf16[16,256,256]{2,1,0:T(8,128)(2,1)}, u32[]{:S(2)}, u32[]{:S(2)}) async-start(bf16[16,256,256]{2,1,0:T(8,128)(2,1)} %bitcast.146), calls=%async_computation.2 | async-start | bytes 4194304 | tf_op jit(solution)/shard_map/all_to_all | solution.py:173
  111.8 127.7 %all-gather.9.cloned.1.call-start = ((), (), s32[]{:S(2)}) async-start(), calls=%async_computation.12 | async-start | bytes 8912896 | tf_op jit(solution)/shard_map/all_gather | solution.py:184
  172.3 179.3 %all-gather.11.cloned.1.call-start = ((), (), s32[]{:S(2)}) async-start(), calls=%async_computation.13 | async-start | bytes 8912896 | tf_op jit(solution)/shard_map/all_gather | solution.py:214
  184.4 0.8 copy-start.4
  187.4 3.1 copy-start.5
  204.8 39.7 %all-to-all-start.4 = ((bf16[16,16,4096]{2,1,0:T(8,128)(2,1)}), bf16[16,16,4096]{2,1,0:T(8,128)(2,1)}, u32[]{:S(2)}, u32[]{:S(2)}) async-start(bf16[16,16,4096]{2,1,0:T(8,128)(2,1)} %broadcast_in_dim.68), calls=%async_computation.4 | async-start | bytes 4194304 | tf_op jit(solution)/shard_map/all_to_all | solution.py:64
  244.5 5.2 %copy-start.10 = (bf16[4096,1024]{0,1:T(8,128)(2,1)S(1)}, bf16[4096,1024]{0,1:T(8,128)(2,1)}, u32[]{:S(2)}) copy-start(bf16[4096,1024]{0,1:T(8,128)(2,1)} %all-gather.9.cloned.1.call-done) | copy-start | bytes 25165828
  244.5 5.3 %copy-start.12 = (f32[256,512]{0,1:T(8,128)S(1)}, f32[256,512]{0,1:T(8,128)}, u32[]{:S(2)}) copy-start(f32[256,512]{0,1:T(8,128)} %fusion.21) | copy-start | bytes 1572868
  249.7 1.5 copy-start.11
  292.5 18.1 %all-to-all-start.6 = ((bf16[4,16,4096]{2,1,0:T(8,128)(2,1)}), bf16[4,16,4096]{2,1,0:T(8,128)(2,1)}, u32[]{:S(2)}, u32[]{:S(2)}) async-start(bf16[4,16,4096]{2,1,0:T(8,128)(2,1)} %broadcast_in_dim.69), calls=%async_computation.6 | async-start | bytes 1048576 | tf_op jit(solution)/shard_map/all_to_all | solution.py:64
  296.7 83.2 %all-gather.13.cloned.1.call-start = ((), (), s32[]{:S(2)}) async-start(), calls=%async_computation.14 | async-start | bytes 2621440 | tf_op jit(solution)/shard_map/all_gather | solution.py:230
  310.6 3.8 copy-start.6
  322.9 20.3 %all-to-all-start.7 = ((bf16[4,640,128]{2,1,0:T(8,128)(2,1)}), bf16[4,640,128]{2,1,0:T(8,128)(2,1)}, u32[]{:S(2)}, u32[]{:S(2)}) async-start(bf16[4,640,128]{2,1,0:T(8,128)(2,1)} %pad_maximum_fusion.2), calls=%async_computation.7 | async-start | bytes 1310720 | tf_op jit(solution)/shard_map/all_to_all | solution.py:249
  392.0 2.6 copy-start.1
  394.7 6.0 %collective-permute-start.3 = (bf16[8,256,512]{2,1,0:T(8,128)(2,1)}, bf16[8,256,512]{2,1,0:T(8,128)(2,1)}, u32[]{:S(2)}, u32[]{:S(2)}) collective-permute-start(bf16[8,256,512]{2,1,0:T(8,128)(2,1)} %dynamic-slice_bitcast_fusion), channel_id=1, source_target_pairs={{0,16},{16,0},{1,17},{17,1},{2,18},{18,2},{3,19},{19,3},{4,20},{20... | collective-permute-start | bytes 6291464 | tf_op jit(solution)/shard_map/ppermute | solution.py:105
  395.3 38.8 %all-to-all-start.8 = ((bf16[16,16,4096]{2,1,0:T(8,128)(2,1)}), bf16[16,16,4096]{2,1,0:T(8,128)(2,1)}, u32[]{:S(2)}, u32[]{:S(2)}) async-start(bf16[16,16,4096]{2,1,0:T(8,128)(2,1)} %bitcast.154), calls=%async_computation.8 | async-start | bytes 4194304 | tf_op jit(solution)/shard_map/all_to_all | solution.py:71
  400.6 70.9 %reduce-scatter.2.cloned.1.call-start = ((), (), s32[]{:S(2)}) async-start(), calls=%async_computation.15 | async-start | bytes 2359296 | tf_op jit(solution)/shard_map/reduce_scatter | solution.py:108
  434.1 34.5 %all-to-all-start.9 = ((bf16[16,16,4096]{2,1,0:T(8,128)(2,1)}), bf16[16,16,4096]{2,1,0:T(8,128)(2,1)}, u32[]{:S(2)}, u32[]{:S(2)}) async-start(bf16[16,16,4096]{2,1,0:T(8,128)(2,1)} %bitcast.149), calls=%async_computation.9 | async-start | bytes 4194304 | tf_op jit(solution)/shard_map/all_to_all | solution.py:71
Sparse Core Ops, SparseCore 0:
  10.6 90.1 all-gather.14
  102.6 69.6 all-gather.6
  174.0 65.4 all-gather.8
  241.7 102.8 all-gather.10
  346.3 33.5 all-gather.12
  409.1 39.1 reduce-scatter.1

commit v2 on v1

--- a/solution.py
+++ b/solution.py
@@ -11,6 +11,7 @@
 SIDE = 4
 DATA = ("z", "core")
 PLANE = ("y", "x")
+ORDER = (0, -1, 1, 2)
 
 
 epsilon = 1e-06
@@ -95,6 +96,18 @@
         )
         heads = lax.dynamic_update_index_in_dim(heads, got, lax.rem(here + SIDE - step, SIDE), 0)
     return heads
+
+
+def ring_shift(piece, step):
+    return lax.ppermute(
+        piece, "y", [(place, (place + step) % SIDE) for place in range(SIDE)]
+    )
+
+
+def ring_parts(piece, before, behind):
+    half = piece.shape[0] // 2
+    opposite = [ring_shift(before[:half], 1), ring_shift(behind[half:], -1)]
+    return jnp.concatenate([piece, before, behind] + opposite, axis=0)
 
 
 def data_sum(partial_rows, after):
@@ -156,7 +169,14 @@
     both_weights = lax.all_gather(
         jnp.concatenate([key_weight, value_weight], axis=1), "y", axis=0, tiled=False
     )
-    output_heads = lax.all_gather(output_weight, "y", axis=0, tiled=True)
+    output_before, output_behind = ring_shift(output_weight, 1), ring_shift(output_weight, -1)
+    here = lax.axis_index("y")
+    ring_heads = lax.rem(here + jnp.array(ORDER, jnp.int32) + SIDE, SIDE)
+    ring_places = jnp.take(
+        jnp.array([ORDER.index(step) for step in (0, 1, 2, -1)], jnp.int32),
+        lax.rem(jnp.arange(SIDE, dtype=jnp.int32) - here + SIDE, SIDE),
+        mode="clip",
+    )
     token_f = tokens.astype(jnp.float32)
     base_scale = rms_scale(token_f)
     normed = (token_f * base_scale).astype(jnp.bfloat16)
@@ -164,9 +184,11 @@
         jnp.bfloat16
     )
     query_heads = heads_of_block(query_rows.reshape(block_count, BLOCK, HD))
-    enc_mine, both_weights, query_heads = lax.optimization_barrier(
-        (enc_mine, both_weights, query_heads)
-    )
+    frozen = jnp.concatenate([up_weight, down_weight.T], axis=1)
+    enc_mine, query_heads, frozen, output_before, output_behind = lax.optimization_barrier(
+        (enc_mine, query_heads, frozen, output_before, output_behind)
+    )
+    output_heads = ring_parts(output_weight, output_before, output_behind)
     features, enc_columns = enc_mine.shape
     keys_here = 2 * NLEN
     block_pieces = jnp.swapaxes(enc_mine.reshape(features, SIDE, keys_here), 0, 1)
@@ -179,8 +201,9 @@
         concat_axis=0,
         tiled=True,
     ).reshape(width, keys_here)
-    frozen = jnp.concatenate([up_weight, down_weight.T], axis=1)
-    enc_block, output_heads, frozen = lax.optimization_barrier((enc_block, output_heads, frozen))
+    enc_block, both_weights, output_heads = lax.optimization_barrier(
+        (enc_block, both_weights, output_heads)
+    )
     frozen_full = lax.all_gather(frozen, DATA, axis=0, tiled=True)
     hidden = up_weight.shape[1]
     up_full = frozen_full[:, :hidden]
@@ -204,7 +227,9 @@
     head_mix = jnp.einsum(
         "hqk,hkd->hqd", attention_b, value_heads, preferred_element_type=jnp.float32
     ).astype(jnp.bfloat16)
-    mix_rows = jnp.swapaxes(head_mix, 0, 1).reshape(BLOCK, SIDE * HD)
+    mix_rows = jnp.swapaxes(
+        jnp.take(head_mix, ring_heads, axis=0, mode="clip"), 0, 1
+    ).reshape(BLOCK, SIDE * HD)
     attn_part = jnp.dot(mix_rows, output_heads, preferred_element_type=jnp.float32)
     rows_share = token_count // tensor_size
     row_start = lax.axis_index(PLANE) * rows_share
@@ -226,10 +251,12 @@
     norm_rows = scatter_sum(norm_part, PLANE)
     out_rows = lax.dynamic_slice_in_dim(grad_output, row_start, rows_share, 0).astype(jnp.float32)
     grad_resid_rows = (out_rows + norm_back(resid_f, resid_scale, norm_rows)).astype(jnp.bfloat16)
-    grad_block = copies_to(grad_resid_rows, "x")
+    grad_block, enc_full = lax.optimization_barrier((copies_to(grad_resid_rows, "x"), enc_full))
     grad_resid = lax.all_gather(grad_block, "y", axis=0, tiled=True)
     grad_mix = contract_last(grad_block, output_heads).astype(jnp.bfloat16)
-    mix_heads_grad = jnp.swapaxes(grad_mix.reshape(BLOCK, SIDE, HD), 0, 1)
+    mix_heads_grad = jnp.take(
+        jnp.swapaxes(grad_mix.reshape(BLOCK, SIDE, HD), 0, 1), ring_places, axis=0, mode="clip"
+    )
     grad_probs = jnp.einsum(
         "hqd,hkd->hqk", mix_heads_grad, value_heads, preferred_element_type=jnp.float32
     )

time: 485 us -> 485 us (level)
  waiting for transfers between devices: 231 us -> 209 us
  local copies, waits for them, and re-layouts: 42.3 us -> 57.6 us
  starting transfers between devices: 40.1 us -> 45.4 us
    all_gather x1 -> x0, waiting for transfers between devices: 57.5 us -> none  [local(): output_heads = lax.all_gather(output_weight, 'y', axis=0, tiled=True)]
    ppermute x0 -> x4, waiting for transfers between devices: none -> 41.2 us  [ring_shift(): lax.ppermute(piece, 'y', [(place, (place + step) % SIDE) for place in ran...]
    all_to_all x1, waiting for transfers between devices: 40.6 us -> 0.01 us  [local(): lax.all_to_all(jnp.take(neighbour_buffer, asked, axis=0, mode='clip'), DA...]
    ppermute x3, waiting for transfers between devices: 2 us -> 38.9 us  [heads_of_block(): lax.ppermute(sent, 'y', [(place, (place + step) % SIDE) for place in rang...]
    all_gather x1, waiting for transfers between devices: 0.01 us -> 34.6 us  [local(): enc_full = lax.all_gather(enc_mine, PLANE, axis=0, tiled=True)]
    all_gather x1, waiting for transfers between devices: 20.9 us -> 2.02 us  [local(): grad_resid = lax.all_gather(grad_block, 'y', axis=0, tiled=True)]
    all_gather x1, waiting for transfers between devices: 11.7 us -> 0.01 us  [local(): lax.all_gather(jnp.concatenate([key_weight, value_weight], axis=1), 'y',...]
    unnamed x32 -> x44, local copies, waits for them, and re-layouts: 6.35 us -> 14.9 us
  transfers between devices with their start and end apart: 17 -> 20, of which waited for: 11 -> 9; matrix products, arithmetic and copies ran while one was open for 22% -> 22% of each run, Pallas kernels for 0% -> 0%
where the time goes in v2:
time: 485 us; the launch traced here: 483 us
  waiting for transfers between devices  209 us (43%)
  blocking collectives  69 us (14%)
  matrix products  58.6 us (12%)
  local copies, waits for them, and re-layouts  57.6 us (12%)
  starting transfers between devices  45.4 us (9%)
  other arithmetic  29.5 us (6%)
  between operations  14.2 us (3%)
    all_to_all x2, waiting for transfers between devices, scatter_sum(): lax.all_to_all(partial_rows.astype(jnp.bfloat16).reshape(size, share, par...  52.3 us
    all_to_all x2, blocking collectives, scatter_sum(): lax.all_to_all(partial_rows.astype(jnp.bfloat16).reshape(size, share, par...  52.2 us
    ppermute x4, waiting for transfers between devices, ring_shift(): lax.ppermute(piece, 'y', [(place, (place + step) % SIDE) for place in ran...  41.2 us
    ppermute x3, waiting for transfers between devices, heads_of_block(): lax.ppermute(sent, 'y', [(place, (place + step) % SIDE) for place in rang...  38.9 us
    all_gather x1, waiting for transfers between devices, local(): enc_full = lax.all_gather(enc_mine, PLANE, axis=0, tiled=True)  34.6 us
    all_gather x1, waiting for transfers between devices, local(): frozen_full = lax.all_gather(frozen, DATA, axis=0, tiled=True)  28.9 us
    dot_general x6, matrix products, contract_first(): lax.dot_general(left_side, right_side, (((0,), (0,)), ((), ())), preferre...  18.2 us
    all_to_all x1, blocking collectives, local(): lax.all_to_all(requests, DATA, split_axis=0, concat_axis=0, tiled=True)  16.8 us
  transfers between devices with their start and end apart: 20, of which 9 were waited for; matrix products, arithmetic and copies ran while one was open for 22% of the time, Pallas kernels for 0%

profile of v2, /device:TPU:1, one launch (start us, length us, event | category | flops | bytes accessed | tf_op | source)
XLA Modules:
  0.0 483.0 jit_solution(6290634639499551688)
XLA Ops:
  7.2 3.2 pad_maximum_fusion.1
  11.7 16.8 %all_to_all.54 = s32[16,1,2]{2,1,0:T(1,128)S(1)} all-to-all(s32[16,1,2]{2,1,0:T(1,128)S(1)} %copy.80), channel_id=1, replica_groups=mesh['z'=8,'core'=2,'y'=4,'x'=4] {'z','core'}, dimensions={0} | all-to-all | bytes 256 | tf_op jit(solution)/shard_map/all_to_all | solution.py:158
  31.8 5.1 %all-to-all-start.1 = ((bf16[16,2,128,256]{3,2,1,0:T(8,128)(2,1)}), bf16[16,2,128,256]{3,2,1,0:T(8,128)(2,1)}, u32[]{:S(2)}, u32[]{:S(2)}) async-start(bf16[16,2,128,256]{3,2,1,0:T(8,128)(2,1)} %bitcast.144), calls=%async_computation.1 | async-start | bytes 4194304 | tf_op jit(solution)/shard_map/all_to_all | solution.py:159
  41.7 2.5 collective-permute-start.1
  49.1 37.5 %collective-permute-done = bf16[64,128]{1,0:T(8,128)(2,1)S(1)} collective-permute-done((bf16[64,128]{1,0:T(8,128)(2,1)}, bf16[64,128]{1,0:T(8,128)(2,1)S(1)}, u32[]{:S(2)}, u32[]{:S(2)}) %collective-permute-start) | collective-permute-done | bytes 16416 | tf_op jit(solution)/shard_map/ppermute | solution.py:94
  88.0 3.0 gather_fusion.1
  92.4 2.3 constant_dynamic-update-slice_fusion.4
  94.7 2.1 copy.83
  96.8 2.6 broadcast_in_dim.76
  99.4 5.7 %all-to-all-start.2 = ((bf16[16,256,256]{2,1,0:T(8,128)(2,1)}), bf16[16,256,256]{2,1,0:T(8,128)(2,1)}, u32[]{:S(2)}, u32[]{:S(2)}) async-start(bf16[16,256,256]{2,1,0:T(8,128)(2,1)} %bitcast.143), calls=%async_computation.2 | async-start | bytes 4194304 | tf_op jit(solution)/shard_map/all_to_all | solution.py:195
  107.6 2.3 constant_dynamic-update-slice_fusion.3
  112.6 2.3 constant_dynamic-update-slice_fusion.2
  114.9 41.2 %collective-permute-done.5 = bf16[64,4096]{1,0:T(8,128)(2,1)S(1)} collective-permute-done((bf16[64,4096]{1,0:T(8,128)(2,1)S(1)}, bf16[64,4096]{1,0:T(8,128)(2,1)S(1)}, u32[]{:S(2)}, u32[]{:S(2)}) %collective-permute-start.5) | collective-permute-done | bytes 524320 | tf_op jit(solution)/shard_map/ppermute | solution.py:102
  157.8 3.1 fusion.49
  161.0 3.5 fusion.46
  164.5 2.4 fusion.43
  166.8 2.4 fusion.40
  173.0 3.0 convolution_convert_fusion.4
  176.1 12.9 %all_to_all.55 = bf16[4,16,4096]{2,1,0:T(8,128)(2,1)S(1)} all-to-all(bf16[4,16,4096]{2,1,0:T(8,128)(2,1)S(1)} %bitcast.150), channel_id=1, replica_groups=mesh['z'=8,'core'=2,'y'=4,'x'=4] {'x'}, dimensions={0} | all-to-all | bytes 1048576 | tf_op jit(solution)/shard_map/all_to_all | solution.py:72
  191.0 4.4 all-to-all-start.4
  195.4 28.9 %all-gather.6.cloned.1.call-done = bf16[4096,1024]{0,1:T(8,128)(2,1)} async-done(((bf16[256,1024]{0,1:T(8,128)(2,1)}), bf16[4096,1024]{0,1:T(8,128)(2,1)}) %all-gather.6.cloned.1.call-update) | async-done | bytes 8388624 | tf_op jit(solution)/shard_map/all_gather | solution.py:207
  224.3 4.9 %fusion.21 = f32[256,512]{0,1:T(8,128)} fusion(bf16[256,4096]{1,0:T(8,128)(2,1)} %param.23, bf16[4096,1024]{0,1:T(8,128)(2,1)} %all-gather.6.cloned.1.call-done), kind=kOutput, calls=%fused_computation.42 | convolution fusion | flops 1073741824 | bytes 6815744 | tf_op jit(solution)/shard_map/dot_general | solution.py:244
  229.3 4.2 fusion.4
  236.1 39.3 %all_to_all.56 = bf16[16,16,4096]{2,1,0:T(8,128)(2,1)S(1)} all-to-all(bf16[16,16,4096]{2,1,0:T(8,128)(2,1)S(1)} %bitcast.153), channel_id=1, replica_groups=mesh['z'=8,'core'=2,'y'=4,'x'=4] {'y','x'}, dimensions={0} | all-to-all | bytes 4194304 | tf_op jit(solution)/shard_map/all_to_all | solution.py:72
  277.8 4.1 all-to-all-start.6
  283.9 10.6 %all-to-all-done.6 = bf16[4,16,4096]{2,1,0:T(8,128)(2,1)} async-done(((bf16[4,16,4096]{2,1,0:T(8,128)(2,1)}), bf16[4,16,4096]{2,1,0:T(8,128)(2,1)}, u32[]{:S(2)}, u32[]{:S(2)}) %all-to-all-start.6) | async-done | bytes 524320 | tf_op jit(solution)/shard_map/all_to_all | solution.py:65
  294.5 34.6 %all-gather.8.cloned.1.call-done = bf16[4096,1024]{0,1:T(8,128)(2,1)} async-done(((bf16[256,1024]{0,1:T(8,128)(2,1)}), bf16[4096,1024]{0,1:T(8,128)(2,1)}) %all-gather.8.cloned.1.call-update) | async-done | bytes 8388624 | tf_op jit(solution)/shard_map/all_gather | solution.py:239
  329.1 3.8 fusion.52
  333.5 2.0 gather_fusion.4
  336.5 2.1 convolution_convert_fusion.7
  344.0 4.4 all-to-all-start.7
  350.3 4.2 copy.111
  354.5 5.0 %convolution_convert_fusion.2 = bf16[256,4096]{1,0:T(8,128)(2,1)} fusion(bf16[4096,1024]{0,1:T(8,128)(2,1)} %all-gather.6.cloned.1.call-done, f32[256,512]{0,1:T(8,128)} %copy-done.15), kind=kOutput, calls=%fused_computation.9 | convolution fusion | flops 1075970048 | bytes 6815744 | tf_op jit(solution)/shard_map/dot_general | solution.py:51
  360.4 3.4 convolution_convert_fusion.6
  363.8 2.3 copy.97
  367.1 7.3 %convolution_convert_fusion.1 = bf16[4096,256]{1,0:T(8,128)(2,1)} fusion(bf16[4096,1024]{0,1:T(8,128)(2,1)} %all-gather.8.cloned.1.call-done, bf16[1024,128]{1,0:T(8,128)(2,1)S(1)} %bitcast.161, bf16[1024,128]{1,0:T(8,128)(2,1)S(1)} %bitcast.160), kind=kOutput, calls=%fused_computation.8 | convolution fusion | flops 2149580800 | bytes 11010048 | tf_op jit(solution)/shard_map/dot_general | solution.py:296
  376.4 4.1 copy.95
  380.5 3.4 convolution_convert_fusion.5
  383.9 2.3 copy.98
  386.2 2.4 pad_maximum_fusion
  391.3 3.1 collective-permute-start.7
  394.4 4.4 all-to-all-start.8
  398.9 4.2 fusion.2
  403.2 4.0 copy.114
  407.2 2.0 convolution_convert_fusion
  409.2 23.7 %all-to-all-done.8 = bf16[16,16,4096]{2,1,0:T(8,128)(2,1)} async-done(((bf16[16,16,4096]{2,1,0:T(8,128)(2,1)}), bf16[16,16,4096]{2,1,0:T(8,128)(2,1)}, u32[]{:S(2)}, u32[]{:S(2)}) %all-to-all-start.8) | async-done | bytes 2097184 | tf_op jit(solution)/shard_map/all_to_all | solution.py:72
  432.8 4.4 all-to-all-start.9
  440.0 28.7 %all-to-all-done.9 = bf16[16,16,4096]{2,1,0:T(8,128)(2,1)} async-done(((bf16[16,16,4096]{2,1,0:T(8,128)(2,1)}), bf16[16,16,4096]{2,1,0:T(8,128)(2,1)}, u32[]{:S(2)}, u32[]{:S(2)}) %all-to-all-start.9) | async-done | bytes 2097184 | tf_op jit(solution)/shard_map/all_to_all | solution.py:72
  (139 shorter events, 62.7 us)
Async XLA Ops:
  7.2 33.0 %copy-start = (bf16[4096,128]{1,0:T(8,128)(2,1)S(1)}, bf16[4096,128]{1,0:T(8,128)(2,1)}, u32[]{:S(2)}) copy-start(bf16[4096,128]{1,0:T(8,128)(2,1)} %param.17) | copy-start | bytes 3145732
  7.2 150.7 %all-gather.12.cloned.1.call-start = ((), (), s32[]{:S(2)}) async-start(), calls=%async_computation.15 | async-start | bytes 10485760 | tf_op jit(solution)/shard_map/all_gather | solution.py:169
  10.4 0.7 copy-start.10
  10.4 0.9 copy-start.11
  10.4 19.4 %copy-start.4 = (bf16[16,128,256]{2,1,0:T(8,128)(2,1)S(1)}, bf16[16,128,256]{2,1,0:T(8,128)(2,1)}, u32[]{:S(2)}) copy-start(bf16[16,128,256]{2,1,0:T(8,128)(2,1)} %param.14) | copy-start | bytes 3145732
  11.5 20.3 %copy-start.12 = (s32[8]{0:T(128)}, s32[8]{0:T(128)S(1)}, u32[]{:S(2)}) copy-start(s32[8]{0:T(128)S(1)} %convert_reduce_fusion.4) | copy-start | bytes 100
  31.8 7.9 %copy-start.3 = (bf16[256,4096]{1,0:T(8,128)(2,1)S(1)}, bf16[256,4096]{1,0:T(8,128)(2,1)}, u32[]{:S(2)}) copy-start(bf16[256,4096]{1,0:T(8,128)(2,1)} %param.13) | copy-start | bytes 6291460
  31.8 56.2 %all-to-all-start.1 = ((bf16[16,2,128,256]{3,2,1,0:T(8,128)(2,1)}), bf16[16,2,128,256]{3,2,1,0:T(8,128)(2,1)}, u32[]{:S(2)}, u32[]{:S(2)}) async-start(bf16[16,2,128,256]{3,2,1,0:T(8,128)(2,1)} %bitcast.144), calls=%async_computation.1 | async-start | bytes 4194304 | tf_op jit(solution)/shard_map/all_to_all | solution.py:159
  36.9 187.5 %all-gather.6.cloned.1.call-start = ((), (), s32[]{:S(2)}) async-start(), calls=%async_computation.11 | async-start | bytes 8912896 | tf_op jit(solution)/shard_map/all_gather | solution.py:207
  36.9 54.2 %collective-permute-start.3 = (bf16[128,4096]{1,0:T(8,128)(2,1)}, bf16[128,4096]{1,0:T(8,128)(2,1)}, u32[]{:S(2)}, u32[]{:S(2)}) collective-permute-start(bf16[128,4096]{1,0:T(8,128)(2,1)} %param.20), channel_id=1, source_target_pairs={{0,4},{4,8},{8,12},{12,0},{1,5},{5,9},{9,13},{13,1},{2,6},{6,10},{... | collective-permute-start | bytes 3145736 | tf_op jit(solution)/shard_map/ppermute | solution.py:102
  38.3 52.8 %collective-permute-start.4 = (bf16[128,4096]{1,0:T(8,128)(2,1)}, bf16[128,4096]{1,0:T(8,128)(2,1)}, u32[]{:S(2)}, u32[]{:S(2)}) collective-permute-start(bf16[128,4096]{1,0:T(8,128)(2,1)} %param.20), channel_id=1, source_target_pairs={{0,12},{4,0},{8,4},{12,8},{1,13},{5,1},{9,5},{13,9},{2,14},{6,2},{... | collective-permute-start | bytes 3145736 | tf_op jit(solution)/shard_map/ppermute | solution.py:102
  41.0 50.2 %copy-start.1 = (s32[4]{0:T(128)S(1)}, s32[4]{0:T(128)}, u32[]{:S(2)}) copy-start(s32[4]{0:T(128)} %constant.109.clone) | copy-start | bytes 52
  41.6 45.0 %collective-permute-start = (bf16[64,128]{1,0:T(8,128)(2,1)}, bf16[64,128]{1,0:T(8,128)(2,1)S(1)}, u32[]{:S(2)}, u32[]{:S(2)}) collective-permute-start(bf16[64,128]{1,0:T(8,128)(2,1)} %get-tuple-element.71), channel_id=1, source_target_pairs={{0,4},{4,8},{8,12},{12,0},{1,5},{5,9},{9,13},{13,1},{2,6},{6,10},{... | collective-permute-start | bytes 49160 | tf_op jit(solution)/shard_map/ppermute | solution.py:94
  41.7 46.3 %collective-permute-start.1 = (bf16[64,128]{1,0:T(8,128)(2,1)}, bf16[64,128]{1,0:T(8,128)(2,1)S(1)}, u32[]{:S(2)}, u32[]{:S(2)}) collective-permute-start(bf16[64,128]{1,0:T(8,128)(2,1)} %get-tuple-element.70), channel_id=1, source_target_pairs={{0,8},{4,12},{8,0},{12,4},{1,9},{5,13},{9,1},{13,5},{2,10},{6,14},... | collective-permute-start | bytes 49160 | tf_op jit(solution)/shard_map/ppermute | solution.py:94
  44.2 43.8 %collective-permute-start.2 = (bf16[64,128]{1,0:T(8,128)(2,1)S(1)}, bf16[64,128]{1,0:T(8,128)(2,1)S(1)}, u32[]{:S(2)}, u32[]{:S(2)}) collective-permute-start(bf16[64,128]{1,0:T(8,128)(2,1)S(1)} %get-tuple-element.69), channel_id=1, source_target_pairs={{0,12},{4,0},{8,4},{12,8},{1,13},{5,1},{9,5},{13,9},{2,14},{6,2},{... | collective-permute-start | bytes 49160 | tf_op jit(solution)/shard_map/ppermute | solution.py:94
  88.0 81.3 %copy-start.6 = (bf16[4,64,128]{2,1,0:T(8,128)(2,1)}, bf16[4,64,128]{2,1,0:T(8,128)(2,1)S(1)}, u32[]{:S(2)}) copy-start(bf16[4,64,128]{2,1,0:T(8,128)(2,1)S(1)} %bitcast_dynamic-update-slice_fusion) | copy-start | bytes 196612
  99.4 58.4 %all-to-all-start.2 = ((bf16[16,256,256]{2,1,0:T(8,128)(2,1)}), bf16[16,256,256]{2,1,0:T(8,128)(2,1)}, u32[]{:S(2)}, u32[]{:S(2)}) async-start(bf16[16,256,256]{2,1,0:T(8,128)(2,1)} %bitcast.143), calls=%async_computation.2 | async-start | bytes 4194304 | tf_op jit(solution)/shard_map/all_to_all | solution.py:195
  105.1 224.0 %all-gather.8.cloned.1.call-start = ((), (), s32[]{:S(2)}) async-start(), calls=%async_computation.12 | async-start | bytes 8912896 | tf_op jit(solution)/shard_map/all_gather | solution.py:239
  106.2 49.9 %collective-permute-start.5 = (bf16[64,4096]{1,0:T(8,128)(2,1)S(1)}, bf16[64,4096]{1,0:T(8,128)(2,1)S(1)}, u32[]{:S(2)}, u32[]{:S(2)}) collective-permute-start(bf16[64,4096]{1,0:T(8,128)(2,1)S(1)} %slice.54), channel_id=1, source_target_pairs={{0,4},{4,8},{8,12},{12,0},{1,5},{5,9},{9,13},{13,1},{2,6},{6,10},{... | collective-permute-start | bytes 1572872 | tf_op jit(solution)/shard_map/ppermute | solution.py:102
  111.0 46.0 %collective-permute-start.6 = (bf16[64,4096]{1,0:T(8,128)(2,1)S(1)}, bf16[64,4096]{1,0:T(8,128)(2,1)S(1)}, u32[]{:S(2)}, u32[]{:S(2)}) collective-permute-start(bf16[64,4096]{1,0:T(8,128)(2,1)S(1)} %slice.55), channel_id=1, source_target_pairs={{0,12},{4,0},{8,4},{12,8},{1,13},{5,1},{9,5},{13,9},{2,14},{6,2},{... | collective-permute-start | bytes 1572872 | tf_op jit(solution)/shard_map/ppermute | solution.py:102
  157.8 6.6 %copy-start.13 = (bf16[16384,256]{1,0:T(8,128)(2,1)S(1)}, bf16[16384,256]{1,0:T(8,128)(2,1)}, u32[]{:S(2)}) copy-start(bf16[16384,256]{1,0:T(8,128)(2,1)} %all-gather.12.cloned.1.call-done) | copy-start | bytes 25165828
  169.3 0.9 copy-start.5
  172.5 3.6 copy-start.8
  191.0 38.3 %all-to-all-start.4 = ((bf16[16,16,4096]{2,1,0:T(8,128)(2,1)}), bf16[16,16,4096]{2,1,0:T(8,128)(2,1)}, u32[]{:S(2)}, u32[]{:S(2)}) async-start(bf16[16,16,4096]{2,1,0:T(8,128)(2,1)} %broadcast_in_dim.78), calls=%async_computation.4 | async-start | bytes 4194304 | tf_op jit(solution)/shard_map/all_to_all | solution.py:65
  229.3 5.2 %copy-start.14 = (bf16[4096,1024]{0,1:T(8,128)(2,1)S(1)}, bf16[4096,1024]{0,1:T(8,128)(2,1)}, u32[]{:S(2)}) copy-start(bf16[4096,1024]{0,1:T(8,128)(2,1)} %all-gather.6.cloned.1.call-done) | copy-start | bytes 25165828
  229.3 5.3 %copy-start.16 = (f32[256,512]{0,1:T(8,128)S(1)}, f32[256,512]{0,1:T(8,128)}, u32[]{:S(2)}) copy-start(f32[256,512]{0,1:T(8,128)} %fusion.21) | copy-start | bytes 1572868
  234.6 1.5 copy-start.15
  277.8 16.6 %all-to-all-start.6 = ((bf16[4,16,4096]{2,1,0:T(8,128)(2,1)}), bf16[4,16,4096]{2,1,0:T(8,128)(2,1)}, u32[]{:S(2)}, u32[]{:S(2)}) async-start(bf16[4,16,4096]{2,1,0:T(8,128)(2,1)} %broadcast_in_dim.79), calls=%async_computation.6 | async-start | bytes 1048576 | tf_op jit(solution)/shard_map/all_to_all | solution.py:65
  282.0 94.5 %all-gather.10.cloned.1.call-start = ((), (), s32[]{:S(2)}) async-start(), calls=%async_computation.13 | async-start | bytes 2621440 | tf_op jit(solution)/shard_map/all_gather | solution.py:255
  329.1 6.5 %copy-start.9 = (bf16[4,64,128]{2,1,0:T(8,128)(2,1)S(1)}, bf16[4,64,128]{2,1,0:T(8,128)(2,1)}, u32[]{:S(2)}) copy-start(bf16[4,64,128]{2,1,0:T(8,128)(2,1)} %copy-done.8) | copy-start | bytes 196612
  332.9 7.0 %copy-start.7 = (bf16[4,64,128]{2,1,0:T(8,128)(2,1)S(1)}, bf16[4,64,128]{2,1,0:T(8,128)(2,1)}, u32[]{:S(2)}) copy-start(bf16[4,64,128]{2,1,0:T(8,128)(2,1)} %copy-done.6) | copy-start | bytes 196612
  344.0 15.5 %all-to-all-start.7 = ((bf16[4,640,128]{2,1,0:T(8,128)(2,1)}), bf16[4,640,128]{2,1,0:T(8,128)(2,1)}, u32[]{:S(2)}, u32[]{:S(2)}) async-start(bf16[4,640,128]{2,1,0:T(8,128)(2,1)} %pad_maximum_fusion.2), calls=%async_computation.7 | async-start | bytes 1310720 | tf_op jit(solution)/shard_map/all_to_all | solution.py:276
  388.6 2.7 copy-start.2
  391.3 7.6 %collective-permute-start.7 = (bf16[8,256,512]{2,1,0:T(8,128)(2,1)}, bf16[8,256,512]{2,1,0:T(8,128)(2,1)}, u32[]{:S(2)}, u32[]{:S(2)}) collective-permute-start(bf16[8,256,512]{2,1,0:T(8,128)(2,1)} %dynamic-slice_bitcast_fusion), channel_id=1, source_target_pairs={{0,16},{16,0},{1,17},{17,1},{2,18},{18,2},{3,19},{19,3},{4,20},{20... | collective-permute-start | bytes 6291464 | tf_op jit(solution)/shard_map/ppermute | solution.py:118
  394.4 38.4 %all-to-all-start.8 = ((bf16[16,16,4096]{2,1,0:T(8,128)(2,1)}), bf16[16,16,4096]{2,1,0:T(8,128)(2,1)}, u32[]{:S(2)}, u32[]{:S(2)}) async-start(bf16[16,16,4096]{2,1,0:T(8,128)(2,1)} %bitcast.151), calls=%async_computation.8 | async-start | bytes 4194304 | tf_op jit(solution)/shard_map/all_to_all | solution.py:72
  398.9 72.7 %reduce-scatter.2.cloned.1.call-start = ((), (), s32[]{:S(2)}) async-start(), calls=%async_computation.14 | async-start | bytes 2359296 | tf_op jit(solution)/shard_map/reduce_scatter | solution.py:121
  432.8 35.8 %all-to-all-start.9 = ((bf16[16,16,4096]{2,1,0:T(8,128)(2,1)}), bf16[16,16,4096]{2,1,0:T(8,128)(2,1)}, u32[]{:S(2)}, u32[]{:S(2)}) async-start(bf16[16,16,4096]{2,1,0:T(8,128)(2,1)} %bitcast.146), calls=%async_computation.9 | async-start | bytes 4194304 | tf_op jit(solution)/shard_map/all_to_all | solution.py:72
Sparse Core Ops, SparseCore 0:
  10.6 145.5 all-gather.11
  157.9 66.4 all-gather.5
  226.8 102.3 all-gather.7
  342.2 34.2 all-gather.9
  407.3 35.8 reduce-scatter.1

commit v3 on v1

--- a/solution.py
+++ b/solution.py
@@ -3,6 +3,8 @@
 import jax
 import jax.numpy as jnp
 from jax import lax
+from jax.experimental import pallas as pl
+from jax.experimental.pallas import tpu as pltpu
 from jax.sharding import PartitionSpec as P
 
 HD = 128
@@ -10,7 +12,8 @@
 NLEN = 128
 SIDE = 4
 DATA = ("z", "core")
-PLANE = ("y", "x")
+PLANE = ("yh", "yl", "x")
+EIGHT = ("yh", "x")
 
 
 epsilon = 1e-06
@@ -78,30 +81,126 @@
     return jnp.sum(swapped.astype(jnp.float32), axis=0)
 
 
-def heads_of_block(own_head_blocks):
-    here = lax.axis_index("y")
-    heads = lax.dynamic_update_index_in_dim(
-        jnp.zeros_like(own_head_blocks),
-        lax.dynamic_index_in_dim(own_head_blocks, here, 0, keepdims=False),
-        here,
-        0,
-    )
-    for step in range(1, SIDE):
-        sent = lax.dynamic_index_in_dim(
-            own_head_blocks, lax.rem(here + step, SIDE), 0, keepdims=False
-        )
-        got = lax.ppermute(
-            sent, "y", [(place, (place + step) % SIDE) for place in range(SIDE)]
-        )
-        heads = lax.dynamic_update_index_in_dim(heads, got, lax.rem(here + SIDE - step, SIDE), 0)
-    return heads
-
-
-def data_sum(partial_rows, after):
-    core = lax.axis_index("core")
-    shares = partial_rows.reshape(lax.axis_size("z"), 2, -1, partial_rows.shape[1])
-    given = lax.dynamic_index_in_dim(shares, 1 - core, 1, keepdims=False)
-    kept = lax.dynamic_index_in_dim(shares, core, 1, keepdims=False)
+def in_pair_order(own, other, axis):
+    first = lax.axis_index("yl") == 0
+    return jnp.where(first, jnp.stack([own, other], axis), jnp.stack([other, own], axis))
+
+
+def pair_swap(given):
+    return lax.ppermute(given, "yl", [(0, 1), (1, 0)])
+
+
+FEATURES = 256
+DEPTH = 512
+
+
+def weight_grads_kernel(
+    core, enc, normed, grad_own, grad_other, both_grads, query_grads, mix_own, mix_other, given, kept
+):
+    step = pl.program_id(0)
+    rows = jnp.concatenate(
+        [
+            contract_first(normed[...], query_grads[...]),
+            jnp.dot(enc[...], both_grads[...], preferred_element_type=jnp.float32),
+            contract_first(grad_own[...], mix_own[...])
+            + contract_first(grad_other[...], mix_other[...]),
+        ],
+        axis=1,
+    ).astype(jnp.bfloat16)
+    mine = lax.rem(step, 2) == core[0]
+
+    @pl.when(mine)
+    def _():
+        kept[0] = rows
+
+    @pl.when(jnp.logical_not(mine))
+    def _():
+        given[0] = rows
+
+
+def weight_grads(enc, normed, grad_own, grad_other, both_grads, query_grads, mix_own, mix_other):
+    width, enc_columns = enc.shape
+    token_count = normed.shape[0]
+    blocks = width // FEATURES
+    columns = both_grads.shape[1] + query_grads.shape[1] + mix_own.shape[1]
+    out_spec = pl.BlockSpec((1, FEATURES, columns), lambda step, core: (step // 2, 0, 0))
+    out_shape = jax.ShapeDtypeStruct((blocks // 2, FEATURES, columns), jnp.bfloat16)
+    return pl.pallas_call(
+        weight_grads_kernel,
+        grid_spec=pltpu.PrefetchScalarGridSpec(
+            num_scalar_prefetch=1,
+            grid=(blocks,),
+            in_specs=[
+                pl.BlockSpec((FEATURES, enc_columns), lambda step, core: (step, 0)),
+                pl.BlockSpec((token_count, FEATURES), lambda step, core: (0, step)),
+                pl.BlockSpec((grad_own.shape[0], FEATURES), lambda step, core: (0, step)),
+                pl.BlockSpec((grad_own.shape[0], FEATURES), lambda step, core: (0, step)),
+                pl.BlockSpec(both_grads.shape, lambda step, core: (0, 0)),
+                pl.BlockSpec(query_grads.shape, lambda step, core: (0, 0)),
+                pl.BlockSpec(mix_own.shape, lambda step, core: (0, 0)),
+                pl.BlockSpec(mix_own.shape, lambda step, core: (0, 0)),
+            ],
+            out_specs=[out_spec, out_spec],
+        ),
+        out_shape=[out_shape, out_shape],
+        cost_estimate=pl.CostEstimate(
+            flops=2 * width * (enc_columns * 2 + token_count * 2) * HD,
+            bytes_accessed=2 * width * (enc_columns + 2 * token_count + columns),
+            transcendentals=0,
+        ),
+        compiler_params=pltpu.CompilerParams(vmem_limit_bytes=24 * 1024 * 1024),
+    )(
+        lax.axis_index("core").astype(jnp.int32).reshape(1),
+        enc,
+        normed,
+        grad_own,
+        grad_other,
+        both_grads,
+        query_grads,
+        mix_own,
+        mix_other,
+    )
+
+
+def project_kernel(enc, weights, out, total):
+    step = pl.program_id(0)
+
+    @pl.when(step == 0)
+    def _():
+        total[...] = jnp.zeros_like(total)
+
+    turned = enc[...].T
+    for head in range(weights.shape[0]):
+        total[head] += jnp.dot(turned, weights[head], preferred_element_type=jnp.float32)
+
+    @pl.when(step == pl.num_programs(0) - 1)
+    def _():
+        out[...] = total[...].astype(out.dtype)
+
+
+def project(enc, weights):
+    width, rows = enc.shape
+    heads, _, columns = weights.shape
+    return pl.pallas_call(
+        project_kernel,
+        grid=(width // DEPTH,),
+        in_specs=[
+            pl.BlockSpec((DEPTH, rows), lambda step: (step, 0)),
+            pl.BlockSpec((heads, DEPTH, columns), lambda step: (0, step, 0)),
+        ],
+        out_specs=pl.BlockSpec((heads, rows, columns), lambda step: (0, 0, 0)),
+        out_shape=jax.ShapeDtypeStruct((heads, rows, columns), jnp.bfloat16),
+        scratch_shapes=[pltpu.VMEM((heads, rows, columns), jnp.float32)],
+        cost_estimate=pl.CostEstimate(
+            flops=2 * width * rows * heads * columns,
+            bytes_accessed=2 * width * (rows + heads * columns),
+            transcendentals=0,
+        ),
+        compiler_params=pltpu.CompilerParams(vmem_limit_bytes=24 * 1024 * 1024),
+    )(enc, weights)
+
+
+def data_sum(given, kept, after):
     got = lax.ppermute(given, "core", [(0, 1), (1, 0)])
     paired = (kept.astype(jnp.float32) + got.astype(jnp.float32)).astype(jnp.bfloat16)
     paired, after = lax.optimization_barrier((paired, after))
@@ -154,43 +253,50 @@
     mine = jnp.take(reply_rows, owners * capacity + slot_index, axis=0, mode="clip")
     enc_mine = mine.reshape(pair_count * NLEN, -1).T
     both_weights = lax.all_gather(
-        jnp.concatenate([key_weight, value_weight], axis=1), "y", axis=0, tiled=False
-    )
-    output_heads = lax.all_gather(output_weight, "y", axis=0, tiled=True)
+        jnp.concatenate([key_weight, value_weight], axis=1), "yl", axis=0, tiled=False
+    )
+    output_heads = lax.all_gather(output_weight, "yl", axis=0, tiled=True)
+    pair_place = lax.axis_index("yl")
     token_f = tokens.astype(jnp.float32)
     base_scale = rms_scale(token_f)
     normed = (token_f * base_scale).astype(jnp.bfloat16)
     query_rows = jnp.dot(normed, query_weight, preferred_element_type=jnp.float32).astype(
         jnp.bfloat16
     )
-    query_heads = heads_of_block(query_rows.reshape(block_count, BLOCK, HD))
-    enc_mine, both_weights, query_heads = lax.optimization_barrier(
-        (enc_mine, both_weights, query_heads)
-    )
+    query_blocks = query_rows.reshape(2, 2, BLOCK, HD)
+
+    def of_class(blocks, axis, place):
+        return lax.dynamic_index_in_dim(blocks, place, axis, keepdims=False)
+
+    query_heads = in_pair_order(
+        of_class(query_blocks, 1, pair_place),
+        pair_swap(of_class(query_blocks, 1, 1 - pair_place)),
+        0,
+    )
+    frozen = jnp.concatenate([up_weight, down_weight.T], axis=1)
+    enc_mine, query_heads, frozen = lax.optimization_barrier((enc_mine, query_heads, frozen))
     features, enc_columns = enc_mine.shape
     keys_here = 2 * NLEN
-    block_pieces = jnp.swapaxes(enc_mine.reshape(features, SIDE, keys_here), 0, 1)
+    class_pieces = enc_mine.reshape(features, 2, 2, keys_here).transpose(2, 0, 1, 3)
     enc_block = lax.all_to_all(
         jnp.broadcast_to(
-            block_pieces[:, None], (SIDE, SIDE, features, keys_here)
-        ).reshape(SIDE * SIDE, features, keys_here),
+            class_pieces.reshape(1, 2, 1, features, 2 * keys_here),
+            (2, 2, SIDE, features, 2 * keys_here),
+        ).reshape(tensor_size, features, 2 * keys_here),
         PLANE,
         split_axis=0,
         concat_axis=0,
         tiled=True,
-    ).reshape(width, keys_here)
-    frozen = jnp.concatenate([up_weight, down_weight.T], axis=1)
-    enc_block, output_heads, frozen = lax.optimization_barrier((enc_block, output_heads, frozen))
+    ).reshape(width, 2 * keys_here)
+    enc_block, both_weights, output_heads = lax.optimization_barrier(
+        (enc_block, both_weights, output_heads)
+    )
     frozen_full = lax.all_gather(frozen, DATA, axis=0, tiled=True)
     hidden = up_weight.shape[1]
     up_full = frozen_full[:, :hidden]
     down_turned = frozen_full[:, hidden:]
-    both_heads = jnp.stack(
-        [
-            contract_first(enc_block, both_weights[head]).astype(jnp.bfloat16)
-            for head in range(SIDE)
-        ]
-    )
+    both_heads = project(enc_block, both_weights).reshape(4, keys_here, 2 * HD)
+    query_heads = query_heads.reshape(4, BLOCK, HD)
     key_heads = both_heads[:, :, :HD]
     value_heads = both_heads[:, :, HD:]
     score_factor = 1.0 / math.sqrt(HD)
@@ -204,13 +310,13 @@
     head_mix = jnp.einsum(
         "hqk,hkd->hqd", attention_b, value_heads, preferred_element_type=jnp.float32
     ).astype(jnp.bfloat16)
-    mix_rows = jnp.swapaxes(head_mix, 0, 1).reshape(BLOCK, SIDE * HD)
+    mix_rows = head_mix.reshape(2, 2, BLOCK, HD).transpose(1, 2, 0, 3).reshape(2 * BLOCK, 2 * HD)
     attn_part = jnp.dot(mix_rows, output_heads, preferred_element_type=jnp.float32)
     rows_share = token_count // tensor_size
     row_start = lax.axis_index(PLANE) * rows_share
     token_rows = lax.dynamic_slice_in_dim(tokens, row_start, rows_share, 0).astype(jnp.float32)
     base_rows = lax.dynamic_slice_in_dim(base_scale, row_start, rows_share, 0)
-    attn_rows, enc_mine = lax.optimization_barrier((scatter_sum(attn_part, "x"), enc_mine))
+    attn_rows, enc_mine = lax.optimization_barrier((scatter_sum(attn_part, EIGHT), enc_mine))
     enc_full = lax.all_gather(enc_mine, PLANE, axis=0, tiled=True)
     resid_f = rounded(token_rows + attn_rows)
     resid_scale = rms_scale(resid_f)
@@ -226,10 +332,14 @@
     norm_rows = scatter_sum(norm_part, PLANE)
     out_rows = lax.dynamic_slice_in_dim(grad_output, row_start, rows_share, 0).astype(jnp.float32)
     grad_resid_rows = (out_rows + norm_back(resid_f, resid_scale, norm_rows)).astype(jnp.bfloat16)
-    grad_block = copies_to(grad_resid_rows, "x")
-    grad_resid = lax.all_gather(grad_block, "y", axis=0, tiled=True)
+    grad_block, enc_full, ffn_part = lax.optimization_barrier(
+        (copies_to(grad_resid_rows, EIGHT), enc_full, ffn_part)
+    )
+    grad_other = pair_swap(grad_block)
     grad_mix = contract_last(grad_block, output_heads).astype(jnp.bfloat16)
-    mix_heads_grad = jnp.swapaxes(grad_mix.reshape(BLOCK, SIDE, HD), 0, 1)
+    mix_heads_grad = (
+        grad_mix.reshape(2, BLOCK, 2, HD).transpose(2, 0, 1, 3).reshape(4, BLOCK, HD)
+    )
     grad_probs = jnp.einsum(
         "hqd,hkd->hqk", mix_heads_grad, value_heads, preferred_element_type=jnp.float32
     )
@@ -246,40 +356,41 @@
     grad_values = jnp.einsum(
         "hqk,hqd->hkd", attention_b, mix_heads_grad, preferred_element_type=jnp.float32
     ).astype(jnp.bfloat16)
-    swapped = lax.all_to_all(
-        jnp.concatenate([grad_keys, grad_values, grad_query, head_mix], axis=1),
-        "y",
-        split_axis=0,
-        concat_axis=0,
-        tiled=True,
-    )
-    swapped, ffn_part = lax.optimization_barrier((swapped, ffn_part))
+    head_grads = jnp.concatenate([grad_keys, grad_values, grad_query, head_mix], axis=1)
+    head_grads, grad_other = lax.optimization_barrier((head_grads, grad_other))
+    head_grads = head_grads.reshape((2, 2) + head_grads.shape[1:])
+    own_grads = of_class(head_grads, 0, pair_place)
+    other_grads = pair_swap(of_class(head_grads, 0, 1 - pair_place))
+    query_from = 2 * keys_here
+    mix_from = query_from + BLOCK
+    swapped = in_pair_order(own_grads[:, :mix_from], other_grads[:, :mix_from], 1)
     both_grads = jnp.concatenate(
         [
-            swapped[:, :keys_here].reshape(enc_columns, HD),
-            swapped[:, keys_here : 2 * keys_here].reshape(enc_columns, HD),
+            swapped[:, :, :keys_here].reshape(enc_columns, HD),
+            swapped[:, :, keys_here:query_from].reshape(enc_columns, HD),
         ],
         axis=1,
     )
-    query_grads = swapped[:, 2 * keys_here : 2 * keys_here + BLOCK].reshape(token_count, HD)
-    mix_back = swapped[:, 2 * keys_here + BLOCK :].reshape(token_count, HD)
-    weight_parts = jnp.concatenate(
-        [
-            contract_first(normed, query_grads),
-            jnp.dot(enc_full, both_grads, preferred_element_type=jnp.float32),
-            contract_first(grad_resid, mix_back),
-        ],
-        axis=1,
-    ).astype(jnp.bfloat16)
-    summed, query_grads = data_sum(weight_parts, query_grads)
+    query_grads = swapped[:, :, query_from:].reshape(token_count, HD)
+    mix_own = own_grads[:, mix_from:].reshape(2 * BLOCK, HD)
+    mix_other = other_grads[:, mix_from:].reshape(2 * BLOCK, HD)
+    given, kept = weight_grads(
+        enc_full, normed, grad_block, grad_other, both_grads, query_grads, mix_own, mix_other
+    )
+    given, kept, ffn_rows_sum = lax.optimization_barrier(
+        (given, kept, scatter_sum(ffn_part, PLANE))
+    )
+    summed, query_grads = data_sum(given, kept, query_grads)
     summed = summed.astype(jnp.float32)
     query_grad = summed[:, :HD]
     key_grad = summed[:, HD : 2 * HD]
     value_grad = summed[:, 2 * HD : 3 * HD]
     mix_grad = summed[:, 3 * HD :].T
-    layer_out = (resid_f + scatter_sum(ffn_part, PLANE)).astype(jnp.bfloat16)
+    layer_out = (resid_f + ffn_rows_sum).astype(jnp.bfloat16)
     input_part = contract_last(query_grads, query_weight)
-    input_rows = scatter_sum(input_part, PLANE)
+    input_rows, query_grad, key_grad, value_grad, mix_grad = lax.optimization_barrier(
+        (scatter_sum(input_part, PLANE), query_grad, key_grad, value_grad, mix_grad)
+    )
     grad_tokens = (
         grad_resid_rows.astype(jnp.float32) + norm_back(token_rows, base_rows, input_rows)
     ).astype(jnp.bfloat16)
@@ -288,7 +399,7 @@
 
 def solution(mesh):
     mesh = jax.sharding.Mesh(
-        mesh.devices.reshape(-1, 2, SIDE, SIDE), DATA + PLANE
+        mesh.devices.reshape(-1, 2, 2, 2, SIDE), DATA + PLANE
     )
     in_specs = (
         P(DATA, None),

time: 485 us -> 483 us (level)
  matrix products: 60.2 us -> 30.3 us
  Pallas kernels: 0 us -> 17.9 us
  waiting for transfers between devices: 231 us -> 238 us
  local copies, waits for them, and re-layouts: 42.3 us -> 47.6 us
    all_gather x3 -> x2, waiting for transfers between devices: 90.2 us -> 26.1 us  [the longest x1 26.1 us: local(): lax.all_gather(jnp.concatenate([key_weight, value_weight], axis=1), 'yl',...]
    ppermute x3, waiting for transfers between devices: 2 us -> 36.8 us  [pair_swap(): return lax.ppermute(given, 'yl', [(0, 1), (1, 0)])]
    all_to_all x2 -> x1, waiting for transfers between devices: 4.7 us -> 36.1 us  [local(): lax.all_to_all(jnp.broadcast_to(class_pieces.reshape(1, 2, 1, features, 2...]
    dot_general x7 -> x0, matrix products: 26 us -> none  [the longest x6 18.7 us: contract_first(): lax.dot_general(left_side, right_side, (((0,), (0,)), ((), ())), preferre...]
    all_gather x1, waiting for transfers between devices: 0.01 us -> 25.7 us  [local(): enc_full = lax.all_gather(enc_mine, PLANE, axis=0, tiled=True)]
    all_to_all x2, waiting for transfers between devices: 50.5 us -> 30.4 us  [scatter_sum(): lax.all_to_all(partial_rows.astype(jnp.bfloat16).reshape(size, share, par...]
    pallas_call x0 -> x2, Pallas kernels: none -> 17.9 us  [the longest x1 11.1 us: weight_grads(): pl.pallas_call(weight_grads_kernel, grid_spec=pltpu.PrefetchScalarGridSpe...]
    all_gather x1, waiting for transfers between devices: 30.1 us -> 17.9 us  [local(): frozen_full = lax.all_gather(frozen, DATA, axis=0, tiled=True)]
  transfers between devices with their start and end apart: 17 -> 15, of which waited for: 11 -> 11; matrix products, arithmetic and copies ran while one was open for 22% -> 15% of each run, Pallas kernels for 0% -> 4%
where the time goes in v3:
time: 483 us; the launch traced here: 480 us
  waiting for transfers between devices  238 us (49%)
  blocking collectives  71.7 us (15%)
  local copies, waits for them, and re-layouts  47.6 us (10%)
  starting transfers between devices  35.9 us (7%)
  matrix products  30.3 us (6%)
  other arithmetic  24.3 us (5%)
  Pallas kernels  17.9 us (4%)
  between operations  14.2 us (3%)
    all_to_all x2, blocking collectives, scatter_sum(): lax.all_to_all(partial_rows.astype(jnp.bfloat16).reshape(size, share, par...  54.9 us
    all_to_all x1, waiting for transfers between devices, local(): lax.all_to_all(jnp.take(neighbour_buffer, asked, axis=0, mode='clip'), DA...  41.6 us
    ppermute x3, waiting for transfers between devices, pair_swap(): return lax.ppermute(given, 'yl', [(0, 1), (1, 0)])  36.8 us
    all_to_all x1, waiting for transfers between devices, local(): lax.all_to_all(jnp.broadcast_to(class_pieces.reshape(1, 2, 1, features, 2...  36.1 us
    all_to_all x2, waiting for transfers between devices, scatter_sum(): lax.all_to_all(partial_rows.astype(jnp.bfloat16).reshape(size, share, par...  30.4 us
    all_gather x1, waiting for transfers between devices, local(): lax.all_gather(jnp.concatenate([key_weight, value_weight], axis=1), 'yl',...  26.1 us
    all_gather x1, waiting for transfers between devices, local(): enc_full = lax.all_gather(enc_mine, PLANE, axis=0, tiled=True)  25.7 us
    all_to_all x2, waiting for transfers between devices, copies_to(): lax.all_to_all(copies, axis, split_axis=0, concat_axis=0, tiled=True)  18.2 us
  transfers between devices with their start and end apart: 15, of which 11 were waited for; matrix products, arithmetic and copies ran while one was open for 15% of the time, Pallas kernels for 4%

profile of v3, /device:TPU:1, one launch (start us, length us, event | category | flops | bytes accessed | tf_op | source)
XLA Modules:
  0.0 479.5 jit_solution(9256031177760847307)
XLA Ops:
  8.0 3.1 pad_maximum_fusion
  12.4 16.8 %all_to_all.49 = s32[16,1,2]{2,1,0:T(1,128)S(1)} all-to-all(s32[16,1,2]{2,1,0:T(1,128)S(1)} %copy.73), channel_id=1, replica_groups=mesh['z'=8,'core'=2,'yh'=2,'yl'=2,'x'=4] {'z','core'}, dimensions={0} | all-to-all | bytes 256 | tf_op jit(solution)/shard_map/all_to_all | solution.py:244
  30.5 2.0 gather_fusion
  32.5 4.9 %all-to-all-start.1 = ((bf16[16,2,128,256]{3,2,1,0:T(8,128)(2,1)}), bf16[16,2,128,256]{3,2,1,0:T(8,128)(2,1)}, u32[]{:S(2)}, u32[]{:S(2)}) async-start(bf16[16,2,128,256]{3,2,1,0:T(8,128)(2,1)} %bitcast.91), calls=%async_computation.1 | async-start | bytes 4194304 | tf_op jit(solution)/shard_map/all_to_all | solution.py:245
  43.1 1.8 pad_maximum_fusion.2
  45.0 41.6 %all-to-all-done.1 = bf16[16,2,128,256]{3,2,1,0:T(8,128)(2,1)} async-done(((bf16[16,2,128,256]{3,2,1,0:T(8,128)(2,1)}), bf16[16,2,128,256]{3,2,1,0:T(8,128)(2,1)}, u32[]{:S(2)}, u32[]{:S(2)}) %all-to-all-start.1) | async-done | bytes 2097184 | tf_op jit(solution)/shard_map/all_to_all | solution.py:245
  86.5 3.0 gather_fusion.1
  89.5 2.1 copy.100
  91.6 2.2 reshape.168
  93.9 2.0 copy.77
  95.9 2.0 copy.78
  97.9 3.4 broadcast_in_dim.51
  101.3 6.8 %all-to-all-start.2 = ((bf16[16,256,512]{2,1,0:T(8,128)(2,1)}), bf16[16,256,512]{2,1,0:T(8,128)(2,1)}, u32[]{:S(2)}, u32[]{:S(2)}) async-start(bf16[16,256,512]{2,1,0:T(8,128)(2,1)} %bitcast.89), calls=%async_computation.2 | async-start | bytes 8388608 | tf_op jit(solution)/shard_map/all_to_all | solution.py:281
  108.2 26.1 %all-gather.12.cloned.1.call-done = bf16[8192,256]{1,0:T(8,128)(2,1)} async-done(((bf16[4096,256]{1,0:T(8,128)(2,1)}), bf16[8192,256]{1,0:T(8,128)(2,1)}) %all-gather.12.cloned.1.call-update) | async-done | bytes 4194320 | tf_op jit(solution)/shard_map/all_gather | solution.py:255
  134.3 36.1 %all-to-all-done.2 = bf16[16,256,512]{2,1,0:T(8,128)(2,1)} async-done(((bf16[16,256,512]{2,1,0:T(8,128)(2,1)}), bf16[16,256,512]{2,1,0:T(8,128)(2,1)}, u32[]{:S(2)}, u32[]{:S(2)}) %all-to-all-start.2) | async-done | bytes 4194336 | tf_op jit(solution)/shard_map/all_to_all | solution.py:281
  170.4 2.2 copy-done.2
  172.6 6.9 %shard_map.154 = bf16[2,512,256]{2,1,0:T(8,128)(2,1)S(1)} custom-call(bf16[4096,512]{1,0:T(8,128)(2,1)} %bitcast.16.enc, bf16[2,4096,256]{2,1,0:T(8,128)(2,1)S(1)} %bitcast.80), custom_call_target="tpu_custom_call" | custom-call | flops 2147483648 | bytes 8388608 | tf_op jit(solution)/shard_map/pallas_call | solution.py:184
  181.9 2.0 convolution_convert_fusion.3
  183.9 19.9 %all_to_all.50 = bf16[8,16,4096]{2,1,0:T(8,128)(2,1)S(1)} all-to-all(bf16[8,16,4096]{2,1,0:T(8,128)(2,1)S(1)} %bitcast.95), channel_id=1, replica_groups=mesh['z'=8,'core'=2,'yh'=2,'yl'=2,'x'=4] {'yh','x'}, dimensions={0} | all-to-all | bytes 2097152 | tf_op jit(solution)/shard_map/all_to_all | solution.py:74
  207.5 4.4 all-to-all-start.4
  211.9 17.9 %all-gather.8.cloned.1.call-done = bf16[4096,1024]{0,1:T(8,128)(2,1)} async-done(((bf16[256,1024]{0,1:T(8,128)(2,1)}), bf16[4096,1024]{0,1:T(8,128)(2,1)}) %all-gather.8.cloned.1.call-update) | async-done | bytes 8388624 | tf_op jit(solution)/shard_map/all_gather | solution.py:294
  229.8 4.9 %fusion.8 = f32[256,512]{0,1:T(8,128)} fusion(bf16[256,4096]{1,0:T(8,128)(2,1)} %param.21, bf16[4096,1024]{0,1:T(8,128)(2,1)} %all-gather.8.cloned.1.call-done), kind=kOutput, calls=%fused_computation.22 | convolution fusion | flops 1073741824 | bytes 6815744 | tf_op jit(solution)/shard_map/dot_general | solution.py:325
  234.8 2.8 all-to-all-done.4
  237.6 4.3 fusion.3
  244.9 35.0 %all_to_all.51 = bf16[16,16,4096]{2,1,0:T(8,128)(2,1)S(1)} all-to-all(bf16[16,16,4096]{2,1,0:T(8,128)(2,1)S(1)} %bitcast.98), channel_id=1, replica_groups=mesh['z'=8,'core'=2,'yh'=2,'yl'=2,'x'=4] {'yh','yl','x'}, dimensions={0} | all-to-all | bytes 4194304 | tf_op jit(solution)/shard_map/all_to_all | solution.py:74
  283.2 4.2 all-to-all-start.6
  287.5 2.0 fusion.56
  289.5 5.1 %convolution_convert_fusion.1 = bf16[256,4096]{1,0:T(8,128)(2,1)} fusion(bf16[4096,1024]{0,1:T(8,128)(2,1)} %all-gather.8.cloned.1.call-done, f32[256,512]{0,1:T(8,128)} %copy-done.17), kind=kOutput, calls=%fused_computation.5 | convolution fusion | flops 1075970048 | bytes 6815744 | tf_op jit(solution)/shard_map/dot_general | solution.py:53
  294.5 15.4 %all-to-all-done.6 = bf16[8,16,4096]{2,1,0:T(8,128)(2,1)} async-done(((bf16[8,16,4096]{2,1,0:T(8,128)(2,1)}), bf16[8,16,4096]{2,1,0:T(8,128)(2,1)}, u32[]{:S(2)}, u32[]{:S(2)}) %all-to-all-start.6) | async-done | bytes 1048608 | tf_op jit(solution)/shard_map/all_to_all | solution.py:67
  309.9 25.7 %all-gather.10.cloned.1.call-done.enc = bf16[4096,1024]{1,0:T(8,128)(2,1)} async-done(((bf16[256,1024]{1,0:T(8,128)(2,1)}), bf16[4096,1024]{1,0:T(8,128)(2,1)}) %all-gather.10.cloned.1.call-update) | async-done | bytes 8388624 | tf_op jit(solution)/shard_map/all_gather | solution.py:320
  335.7 2.8 convolution_convert_fusion.6
  339.9 5.4 %all-to-all-start.7 = ((bf16[16,16,4096]{2,1,0:T(8,128)(2,1)}), bf16[16,16,4096]{2,1,0:T(8,128)(2,1)}, u32[]{:S(2)}, u32[]{:S(2)}) async-start(bf16[16,16,4096]{2,1,0:T(8,128)(2,1)} %bitcast.97), calls=%async_computation.7 | async-start | bytes 4194304 | tf_op jit(solution)/shard_map/all_to_all | solution.py:74
  347.6 2.1 convolution_convert_fusion.4
  351.9 27.8 %collective-permute-done.1.grad_other = bf16[128,4096]{1,0:T(8,128)(2,1)} collective-permute-done((bf16[128,4096]{1,0:T(8,128)(2,1)}, bf16[128,4096]{1,0:T(8,128)(2,1)}, u32[]{:S(2)}, u32[]{:S(2)}) %collective-permute-start.1) | collective-permute-done | bytes 1048608 | tf_op jit(solution)/shard_map/ppermute | solution.py:90
  383.3 9.1 %collective-permute-done.2 = bf16[2,640,128]{2,1,0:T(8,128)(2,1)} collective-permute-done((bf16[2,640,128]{2,1,0:T(8,128)(2,1)}, bf16[2,640,128]{2,1,0:T(8,128)(2,1)}, u32[]{:S(2)}, u32[]{:S(2)}) %collective-permute-start.2) | collective-permute-done | bytes 327712 | tf_op jit(solution)/shard_map/ppermute | solution.py:90
  394.4 3.4 copy-done.1
  397.8 11.1 %shard_map.155 = (bf16[8,256,512]{2,1,0:T(8,128)(2,1)S(1)}, bf16[8,256,512]{2,1,0:T(8,128)(2,1)S(1)}) custom-call(s32[1]{0:T(128)} %bitcast.22.core, bf16[4096,1024]{1,0:T(8,128)(2,1)S(1)} %copy-done.1, bf16[256,4096]{1,0:T(8,128)(2,1)S(1)} %fusion.1.normed, bf16[128,4096]{1,0:T(8,128)(2,1)} %bitcast.26.grad_own, ...), custom_call_target="tpu_custom_call" | custom-call | flops 2684354560 | bytes 16777216 | tf_op jit(solution)/shard_map/pallas_call | solution.py:128
  411.5 2.8 convert_reduce_fusion.1
  414.3 1.5 collective-permute-start.3
  415.8 4.0 collective-permute-done.3
  419.8 1.9 add_convert_fusion
  421.7 4.0 copy.91
  425.7 2.0 convolution_convert_fusion
  427.7 5.2 %all-to-all-start.8 = ((bf16[16,16,4096]{2,1,0:T(8,128)(2,1)}), bf16[16,16,4096]{2,1,0:T(8,128)(2,1)S(1)}, u32[]{:S(2)}, u32[]{:S(2)}) async-start(bf16[16,16,4096]{2,1,0:T(8,128)(2,1)} %bitcast.92), calls=%async_computation.8 | async-start | bytes 4194304 | tf_op jit(solution)/shard_map/all_to_all | solution.py:74
  433.0 1.6 fusion.39
  434.6 30.4 %all-to-all-done.8 = bf16[16,16,4096]{2,1,0:T(8,128)(2,1)S(1)} async-done(((bf16[16,16,4096]{2,1,0:T(8,128)(2,1)}), bf16[16,16,4096]{2,1,0:T(8,128)(2,1)S(1)}, u32[]{:S(2)}, u32[]{:S(2)}) %all-to-all-start.8) | async-done | bytes 2097184 | tf_op jit(solution)/shard_map/all_to_all | solution.py:74
  466.3 1.6 fusion.76
  469.0 1.7 fusion.31
  (118 shorter events, 40.3 us)
Async XLA Ops:
  7.2 32.5 %copy-start = (bf16[4096,128]{1,0:T(8,128)(2,1)S(1)}, bf16[4096,128]{1,0:T(8,128)(2,1)}, u32[]{:S(2)}) copy-start(bf16[4096,128]{1,0:T(8,128)(2,1)} %param.15) | copy-start | bytes 3145732
  7.2 101.0 %all-gather.6.cloned.1.call-start = ((), (), s32[]{:S(2)}) async-start(), calls=%async_computation.10 | async-start | bytes 3145728 | tf_op jit(solution)/shard_map/all_gather | solution.py:258
  7.9 126.3 %all-gather.12.cloned.1.call-start = ((), (), s32[]{:S(2)}) async-start(), calls=%async_computation.14 | async-start | bytes 6291456 | tf_op jit(solution)/shard_map/all_gather | solution.py:255
  11.1 0.7 copy-start.14
  11.1 0.9 copy-start.15
  11.1 19.4 %copy-start.9 = (bf16[16,128,256]{2,1,0:T(8,128)(2,1)S(1)}, bf16[16,128,256]{2,1,0:T(8,128)(2,1)}, u32[]{:S(2)}) copy-start(bf16[16,128,256]{2,1,0:T(8,128)(2,1)} %param.12) | copy-start | bytes 3145732
  32.5 5.0 %copy-start.7 = (bf16[256,4096]{1,0:T(8,128)(2,1)S(1)}, bf16[256,4096]{1,0:T(8,128)(2,1)}, u32[]{:S(2)}) copy-start(bf16[256,4096]{1,0:T(8,128)(2,1)} %param.11) | copy-start | bytes 6291460
  32.5 54.0 %all-to-all-start.1 = ((bf16[16,2,128,256]{3,2,1,0:T(8,128)(2,1)}), bf16[16,2,128,256]{3,2,1,0:T(8,128)(2,1)}, u32[]{:S(2)}, u32[]{:S(2)}) async-start(bf16[16,2,128,256]{3,2,1,0:T(8,128)(2,1)} %bitcast.91), calls=%async_computation.1 | async-start | bytes 4194304 | tf_op jit(solution)/shard_map/all_to_all | solution.py:245
  37.5 192.4 %all-gather.8.cloned.1.call-start = ((), (), s32[]{:S(2)}) async-start(), calls=%async_computation.11 | async-start | bytes 8912896 | tf_op jit(solution)/shard_map/all_gather | solution.py:294
  37.5 1.6 copy-start.8
  40.4 4.5 collective-permute-start
  101.3 69.1 %all-to-all-start.2 = ((bf16[16,256,512]{2,1,0:T(8,128)(2,1)}), bf16[16,256,512]{2,1,0:T(8,128)(2,1)}, u32[]{:S(2)}, u32[]{:S(2)}) async-start(bf16[16,256,512]{2,1,0:T(8,128)(2,1)} %bitcast.89), calls=%async_computation.2 | async-start | bytes 8388608 | tf_op jit(solution)/shard_map/all_to_all | solution.py:281
  108.1 227.6 %all-gather.10.cloned.1.call-start = ((), (), s32[]{:S(2)}) async-start(), calls=%async_computation.12 | async-start | bytes 8912896 | tf_op jit(solution)/shard_map/all_gather | solution.py:320
  170.4 2.2 copy-start.2
  179.4 0.8 copy-start.3
  180.5 1.3 copy-start.13
  207.5 30.1 %all-to-all-start.4 = ((bf16[16,16,4096]{2,1,0:T(8,128)(2,1)}), bf16[16,16,4096]{2,1,0:T(8,128)(2,1)}, u32[]{:S(2)}, u32[]{:S(2)}) async-start(bf16[16,16,4096]{2,1,0:T(8,128)(2,1)} %broadcast_in_dim.52), calls=%async_computation.4 | async-start | bytes 4194304 | tf_op jit(solution)/shard_map/all_to_all | solution.py:67
  237.6 5.8 %copy-start.16 = (bf16[4096,1024]{0,1:T(8,128)(2,1)S(1)}, bf16[4096,1024]{0,1:T(8,128)(2,1)}, u32[]{:S(2)}) copy-start(bf16[4096,1024]{0,1:T(8,128)(2,1)} %all-gather.8.cloned.1.call-done) | copy-start | bytes 25165828
  237.6 5.8 %copy-start.18 = (f32[256,512]{0,1:T(8,128)S(1)}, f32[256,512]{0,1:T(8,128)}, u32[]{:S(2)}) copy-start(f32[256,512]{0,1:T(8,128)} %fusion.8) | copy-start | bytes 1572868
  243.4 1.5 copy-start.17
  281.5 0.7 copy-start.10
  283.2 26.7 %all-to-all-start.6 = ((bf16[8,16,4096]{2,1,0:T(8,128)(2,1)}), bf16[8,16,4096]{2,1,0:T(8,128)(2,1)}, u32[]{:S(2)}, u32[]{:S(2)}) async-start(bf16[8,16,4096]{2,1,0:T(8,128)(2,1)} %broadcast_in_dim.53), calls=%async_computation.6 | async-start | bytes 2097152 | tf_op jit(solution)/shard_map/all_to_all | solution.py:67
  338.4 41.3 %collective-permute-start.1 = (bf16[128,4096]{1,0:T(8,128)(2,1)}, bf16[128,4096]{1,0:T(8,128)(2,1)}, u32[]{:S(2)}, u32[]{:S(2)}) collective-permute-start(bf16[128,4096]{1,0:T(8,128)(2,1)} %bitcast.26.grad_own), channel_id=1, source_target_pairs={{0,4},{4,0},{1,5},{5,1},{2,6},{6,2},{3,7},{7,3},{8,12},{12,8},{9,1... | collective-permute-start | bytes 3145736 | tf_op jit(solution)/shard_map/ppermute | solution.py:90
  339.3 0.6 copy-start.12
  339.9 71.6 %all-to-all-start.7 = ((bf16[16,16,4096]{2,1,0:T(8,128)(2,1)}), bf16[16,16,4096]{2,1,0:T(8,128)(2,1)}, u32[]{:S(2)}, u32[]{:S(2)}) async-start(bf16[16,16,4096]{2,1,0:T(8,128)(2,1)} %bitcast.97), calls=%async_computation.7 | async-start | bytes 4194304 | tf_op jit(solution)/shard_map/all_to_all | solution.py:74
  345.3 120.0 %reduce-scatter.2.cloned.1.call-start = ((), (), s32[]{:S(2)}) async-start(), calls=%async_computation.13 | async-start | bytes 2359296 | tf_op jit(solution)/shard_map/reduce_scatter | solution.py:207
  380.6 11.8 %collective-permute-start.2 = (bf16[2,640,128]{2,1,0:T(8,128)(2,1)}, bf16[2,640,128]{2,1,0:T(8,128)(2,1)}, u32[]{:S(2)}, u32[]{:S(2)}) collective-permute-start(bf16[2,640,128]{2,1,0:T(8,128)(2,1)} %get-tuple-element.81), channel_id=1, source_target_pairs={{0,4},{4,0},{1,5},{5,1},{2,6},{6,2},{3,7},{7,3},{8,12},{12,8},{9,1... | collective-permute-start | bytes 983048 | tf_op jit(solution)/shard_map/ppermute | solution.py:90
  394.4 3.4 copy-start.1
  408.9 1.3 copy-start.4
  410.2 1.3 copy-start.6
  411.5 8.3 %copy-start.5 = (bf16[8,256,512]{2,1,0:T(8,128)(2,1)S(1)}, bf16[8,256,512]{2,1,0:T(8,128)(2,1)}, u32[]{:S(2)}) copy-start(bf16[8,256,512]{2,1,0:T(8,128)(2,1)} %copy-done.4) | copy-start | bytes 6291460
  414.3 5.5 %collective-permute-start.3 = (bf16[8,256,512]{2,1,0:T(8,128)(2,1)}, bf16[8,256,512]{2,1,0:T(8,128)(2,1)S(1)}, u32[]{:S(2)}, u32[]{:S(2)}) collective-permute-start(bf16[8,256,512]{2,1,0:T(8,128)(2,1)} %copy-done.6), channel_id=1, source_target_pairs={{0,16},{16,0},{1,17},{17,1},{2,18},{18,2},{3,19},{19,3},{4,20},{20... | collective-permute-start | bytes 6291464 | tf_op jit(solution)/shard_map/ppermute | solution.py:204
  427.7 37.2 %all-to-all-start.8 = ((bf16[16,16,4096]{2,1,0:T(8,128)(2,1)}), bf16[16,16,4096]{2,1,0:T(8,128)(2,1)S(1)}, u32[]{:S(2)}, u32[]{:S(2)}) async-start(bf16[16,16,4096]{2,1,0:T(8,128)(2,1)} %bitcast.92), calls=%async_computation.8 | async-start | bytes 4194304 | tf_op jit(solution)/shard_map/all_to_all | solution.py:74
  434.6 34.4 %copy-start.11 = (bf16[16,4096]{1,0:T(8,128)(2,1)S(1)}, bf16[16,4096]{1,0:T(8,128)(2,1)}, u32[]{:S(2)}) copy-start(bf16[16,4096]{1,0:T(8,128)(2,1)} %copy-done.10) | copy-start | bytes 393220
Sparse Core Ops, SparseCore 0:
  9.8 42.6 all-gather.5
  54.4 79.8 all-gather.11
  136.0 93.7 all-gather.7
  232.1 103.5 all-gather.9
  425.9 37.1 reduce-scatter.1

commit v4 on v3

--- a/solution.py
+++ b/solution.py
@@ -90,23 +90,23 @@
     return lax.ppermute(given, "yl", [(0, 1), (1, 0)])
 
 
-FEATURES = 256
-DEPTH = 512
-
-
 def weight_grads_kernel(
     core, enc, normed, grad_own, grad_other, both_grads, query_grads, mix_own, mix_other, given, kept
 ):
     step = pl.program_id(0)
-    rows = jnp.concatenate(
+
+    def times(left, right):
+        return jnp.dot(left, right, preferred_element_type=jnp.float32)
+
+    turned = jnp.concatenate(
         [
-            contract_first(normed[...], query_grads[...]),
-            jnp.dot(enc[...], both_grads[...], preferred_element_type=jnp.float32),
-            contract_first(grad_own[...], mix_own[...])
-            + contract_first(grad_other[...], mix_other[...]),
+            times(query_grads[...], normed[...]),
+            times(both_grads[...], enc[0]),
+            times(mix_own[...], grad_own[...]) + times(mix_other[...], grad_other[...]),
         ],
-        axis=1,
-    ).astype(jnp.bfloat16)
+        axis=0,
+    )
+    rows = turned.T.astype(jnp.bfloat16)
     mine = lax.rem(step, 2) == core[0]
 
     @pl.when(mine)
@@ -119,33 +119,30 @@
 
 
 def weight_grads(enc, normed, grad_own, grad_other, both_grads, query_grads, mix_own, mix_other):
-    width, enc_columns = enc.shape
+    blocks, enc_rows, features = enc.shape
     token_count = normed.shape[0]
-    blocks = width // FEATURES
-    columns = both_grads.shape[1] + query_grads.shape[1] + mix_own.shape[1]
-    out_spec = pl.BlockSpec((1, FEATURES, columns), lambda step, core: (step // 2, 0, 0))
-    out_shape = jax.ShapeDtypeStruct((blocks // 2, FEATURES, columns), jnp.bfloat16)
+    columns = both_grads.shape[0] + query_grads.shape[0] + mix_own.shape[0]
+    out_spec = pl.BlockSpec((1, features, columns), lambda step, core: (step // 2, 0, 0))
+    out_shape = jax.ShapeDtypeStruct((blocks // 2, features, columns), jnp.bfloat16)
+    small = [both_grads, query_grads, mix_own, mix_other]
     return pl.pallas_call(
         weight_grads_kernel,
         grid_spec=pltpu.PrefetchScalarGridSpec(
             num_scalar_prefetch=1,
             grid=(blocks,),
             in_specs=[
-                pl.BlockSpec((FEATURES, enc_columns), lambda step, core: (step, 0)),
-                pl.BlockSpec((token_count, FEATURES), lambda step, core: (0, step)),
-                pl.BlockSpec((grad_own.shape[0], FEATURES), lambda step, core: (0, step)),
-                pl.BlockSpec((grad_own.shape[0], FEATURES), lambda step, core: (0, step)),
-                pl.BlockSpec(both_grads.shape, lambda step, core: (0, 0)),
-                pl.BlockSpec(query_grads.shape, lambda step, core: (0, 0)),
-                pl.BlockSpec(mix_own.shape, lambda step, core: (0, 0)),
-                pl.BlockSpec(mix_own.shape, lambda step, core: (0, 0)),
-            ],
+                pl.BlockSpec((1, enc_rows, features), lambda step, core: (step, 0, 0)),
+                pl.BlockSpec((token_count, features), lambda step, core: (0, step)),
+                pl.BlockSpec((grad_own.shape[0], features), lambda step, core: (0, step)),
+                pl.BlockSpec((grad_own.shape[0], features), lambda step, core: (0, step)),
+            ]
+            + [pl.BlockSpec(part.shape, lambda step, core: (0, 0)) for part in small],
             out_specs=[out_spec, out_spec],
         ),
         out_shape=[out_shape, out_shape],
         cost_estimate=pl.CostEstimate(
-            flops=2 * width * (enc_columns * 2 + token_count * 2) * HD,
-            bytes_accessed=2 * width * (enc_columns + 2 * token_count + columns),
+            flops=2 * blocks * features * (enc_rows * 2 + token_count * 2) * HD,
+            bytes_accessed=2 * blocks * features * (enc_rows + 2 * token_count + columns),
             transcendentals=0,
         ),
         compiler_params=pltpu.CompilerParams(vmem_limit_bytes=24 * 1024 * 1024),
@@ -155,58 +152,54 @@
         normed,
         grad_own,
         grad_other,
-        both_grads,
-        query_grads,
-        mix_own,
-        mix_other,
-    )
-
-
-def project_kernel(enc, weights, out, total):
+        *small,
+    )
+
+
+def project_kernel(enc, first_weights, second_weights, out, total):
     step = pl.program_id(0)
 
     @pl.when(step == 0)
     def _():
         total[...] = jnp.zeros_like(total)
 
-    turned = enc[...].T
-    for head in range(weights.shape[0]):
-        total[head] += jnp.dot(turned, weights[head], preferred_element_type=jnp.float32)
+    total[0] += jnp.dot(enc[0], first_weights[...], preferred_element_type=jnp.float32)
+    total[1] += jnp.dot(enc[0], second_weights[...], preferred_element_type=jnp.float32)
 
     @pl.when(step == pl.num_programs(0) - 1)
     def _():
         out[...] = total[...].astype(out.dtype)
 
 
-def project(enc, weights):
-    width, rows = enc.shape
-    heads, _, columns = weights.shape
+def project(enc, first_weights, second_weights):
+    blocks, rows, features = enc.shape
+    columns = first_weights.shape[1]
+    weight_spec = pl.BlockSpec((features, columns), lambda step: (step, 0))
     return pl.pallas_call(
         project_kernel,
-        grid=(width // DEPTH,),
+        grid=(blocks,),
         in_specs=[
-            pl.BlockSpec((DEPTH, rows), lambda step: (step, 0)),
-            pl.BlockSpec((heads, DEPTH, columns), lambda step: (0, step, 0)),
+            pl.BlockSpec((1, rows, features), lambda step: (step, 0, 0)),
+            weight_spec,
+            weight_spec,
         ],
-        out_specs=pl.BlockSpec((heads, rows, columns), lambda step: (0, 0, 0)),
-        out_shape=jax.ShapeDtypeStruct((heads, rows, columns), jnp.bfloat16),
-        scratch_shapes=[pltpu.VMEM((heads, rows, columns), jnp.float32)],
+        out_specs=pl.BlockSpec((2, rows, columns), lambda step: (0, 0, 0)),
+        out_shape=jax.ShapeDtypeStruct((2, rows, columns), jnp.bfloat16),
+        scratch_shapes=[pltpu.VMEM((2, rows, columns), jnp.float32)],
         cost_estimate=pl.CostEstimate(
-            flops=2 * width * rows * heads * columns,
-            bytes_accessed=2 * width * (rows + heads * columns),
+            flops=4 * blocks * features * rows * columns,
+            bytes_accessed=2 * blocks * features * (rows + 2 * columns),
             transcendentals=0,
         ),
         compiler_params=pltpu.CompilerParams(vmem_limit_bytes=24 * 1024 * 1024),
-    )(enc, weights)
+    )(enc, first_weights, second_weights)
 
 
 def data_sum(given, kept, after):
     got = lax.ppermute(given, "core", [(0, 1), (1, 0)])
     paired = (kept.astype(jnp.float32) + got.astype(jnp.float32)).astype(jnp.bfloat16)
     paired, after = lax.optimization_barrier((paired, after))
-    summed = lax.psum_scatter(
-        paired.reshape(-1, paired.shape[2]), "z", scatter_dimension=0, tiled=True
-    )
+    summed = lax.psum_scatter(paired, "z", scatter_dimension=0, tiled=False)
     return summed, after
 
 
@@ -251,11 +244,10 @@
     )
     reply_rows = replies.reshape((data_size * capacity,) + replies.shape[2:])
     mine = jnp.take(reply_rows, owners * capacity + slot_index, axis=0, mode="clip")
-    enc_mine = mine.reshape(pair_count * NLEN, -1).T
-    both_weights = lax.all_gather(
-        jnp.concatenate([key_weight, value_weight], axis=1), "yl", axis=0, tiled=False
-    )
-    output_heads = lax.all_gather(output_weight, "yl", axis=0, tiled=True)
+    enc_mine = mine.reshape(pair_count * NLEN, -1)
+    both_weights = jnp.concatenate([key_weight, value_weight], axis=1)
+    pair_weights = pair_swap(both_weights)
+    pair_output = pair_swap(output_weight)
     pair_place = lax.axis_index("yl")
     token_f = tokens.astype(jnp.float32)
     base_scale = rms_scale(token_f)
@@ -268,34 +260,38 @@
     def of_class(blocks, axis, place):
         return lax.dynamic_index_in_dim(blocks, place, axis, keepdims=False)
 
-    query_heads = in_pair_order(
-        of_class(query_blocks, 1, pair_place),
-        pair_swap(of_class(query_blocks, 1, 1 - pair_place)),
-        0,
+    query_heads = jnp.stack(
+        [
+            of_class(query_blocks, 1, pair_place),
+            pair_swap(of_class(query_blocks, 1, 1 - pair_place)),
+        ]
     )
     frozen = jnp.concatenate([up_weight, down_weight.T], axis=1)
-    enc_mine, query_heads, frozen = lax.optimization_barrier((enc_mine, query_heads, frozen))
-    features, enc_columns = enc_mine.shape
+    enc_mine, query_heads, frozen, pair_weights, pair_output = lax.optimization_barrier(
+        (enc_mine, query_heads, frozen, pair_weights, pair_output)
+    )
+    output_heads = jnp.concatenate([output_weight, pair_output], axis=0)
+    enc_columns, features = enc_mine.shape
     keys_here = 2 * NLEN
-    class_pieces = enc_mine.reshape(features, 2, 2, keys_here).transpose(2, 0, 1, 3)
+    class_pieces = jnp.swapaxes(enc_mine.reshape(2, 2, keys_here, features), 0, 1)
     enc_block = lax.all_to_all(
         jnp.broadcast_to(
-            class_pieces.reshape(1, 2, 1, features, 2 * keys_here),
-            (2, 2, SIDE, features, 2 * keys_here),
-        ).reshape(tensor_size, features, 2 * keys_here),
+            class_pieces.reshape(1, 2, 1, 2 * keys_here, features),
+            (2, 2, SIDE, 2 * keys_here, features),
+        ).reshape(tensor_size, 2 * keys_here, features),
         PLANE,
         split_axis=0,
         concat_axis=0,
         tiled=True,
-    ).reshape(width, 2 * keys_here)
-    enc_block, both_weights, output_heads = lax.optimization_barrier(
-        (enc_block, both_weights, output_heads)
+    )
+    enc_block, output_heads, enc_mine = lax.optimization_barrier(
+        (enc_block, output_heads, enc_mine)
     )
     frozen_full = lax.all_gather(frozen, DATA, axis=0, tiled=True)
     hidden = up_weight.shape[1]
     up_full = frozen_full[:, :hidden]
     down_turned = frozen_full[:, hidden:]
-    both_heads = project(enc_block, both_weights).reshape(4, keys_here, 2 * HD)
+    both_heads = project(enc_block, both_weights, pair_weights).reshape(4, keys_here, 2 * HD)
     query_heads = query_heads.reshape(4, BLOCK, HD)
     key_heads = both_heads[:, :, :HD]
     value_heads = both_heads[:, :, HD:]
@@ -317,7 +313,7 @@
     token_rows = lax.dynamic_slice_in_dim(tokens, row_start, rows_share, 0).astype(jnp.float32)
     base_rows = lax.dynamic_slice_in_dim(base_scale, row_start, rows_share, 0)
     attn_rows, enc_mine = lax.optimization_barrier((scatter_sum(attn_part, EIGHT), enc_mine))
-    enc_full = lax.all_gather(enc_mine, PLANE, axis=0, tiled=True)
+    enc_full = lax.all_gather(enc_mine, PLANE, axis=0, tiled=False)
     resid_f = rounded(token_rows + attn_rows)
     resid_scale = rms_scale(resid_f)
     ffn_in = copies_to((resid_f * resid_scale).astype(jnp.bfloat16), PLANE)
@@ -357,10 +353,13 @@
         "hqk,hqd->hkd", attention_b, mix_heads_grad, preferred_element_type=jnp.float32
     ).astype(jnp.bfloat16)
     head_grads = jnp.concatenate([grad_keys, grad_values, grad_query, head_mix], axis=1)
-    head_grads, grad_other = lax.optimization_barrier((head_grads, grad_other))
+    head_grads, grad_other, ffn_part = lax.optimization_barrier(
+        (head_grads, grad_other, ffn_part)
+    )
+    ffn_rows_sum = scatter_sum(ffn_part, PLANE)
     head_grads = head_grads.reshape((2, 2) + head_grads.shape[1:])
-    own_grads = of_class(head_grads, 0, pair_place)
-    other_grads = pair_swap(of_class(head_grads, 0, 1 - pair_place))
+    own_grads = head_grads[0]
+    other_grads = pair_swap(head_grads[1])
     query_from = 2 * keys_here
     mix_from = query_from + BLOCK
     swapped = in_pair_order(own_grads[:, :mix_from], other_grads[:, :mix_from], 1)
@@ -375,11 +374,16 @@
     mix_own = own_grads[:, mix_from:].reshape(2 * BLOCK, HD)
     mix_other = other_grads[:, mix_from:].reshape(2 * BLOCK, HD)
     given, kept = weight_grads(
-        enc_full, normed, grad_block, grad_other, both_grads, query_grads, mix_own, mix_other
-    )
-    given, kept, ffn_rows_sum = lax.optimization_barrier(
-        (given, kept, scatter_sum(ffn_part, PLANE))
-    )
+        enc_full,
+        normed,
+        grad_block,
+        grad_other,
+        both_grads.T,
+        query_grads.T,
+        mix_own.T,
+        mix_other.T,
+    )
+    given, kept, ffn_rows_sum = lax.optimization_barrier((given, kept, ffn_rows_sum))
     summed, query_grads = data_sum(given, kept, query_grads)
     summed = summed.astype(jnp.float32)
     query_grad = summed[:, :HD]

time: 483 us -> 508 us (1.052)
  blocking collectives: 71.7 us -> 92.9 us
  waiting for transfers between devices: 238 us -> 229 us
  Pallas kernels: 17.9 us -> 23 us
    ppermute x3 -> x5, waiting for transfers between devices: 36.8 us -> 101 us  [pair_swap(): return lax.ppermute(given, 'yl', [(0, 1), (1, 0)])]
    all_gather x3 -> x1, waiting for transfers between devices: 51.8 us -> 0.01 us  [local(): enc_full = lax.all_gather(enc_mine, PLANE, axis=0, tiled=False)]
    all_to_all x1, waiting for transfers between devices: 41.6 us -> 0.01 us  [local(): lax.all_to_all(jnp.take(neighbour_buffer, asked, axis=0, mode='clip'), DA...]
    all_to_all x1, waiting for transfers between devices: 36.1 us -> 58.3 us  [local(): lax.all_to_all(jnp.broadcast_to(class_pieces.reshape(1, 2, 1, 2 * keys_he...]
    all_to_all x2, blocking collectives: 54.9 us -> 76.1 us  [scatter_sum(): lax.all_to_all(partial_rows.astype(jnp.bfloat16).reshape(size, share, par...]
    all_to_all x2, waiting for transfers between devices: 18.2 us -> 36.2 us  [copies_to(): lax.all_to_all(copies, axis, split_axis=0, concat_axis=0, tiled=True)]
    all_gather x1, waiting for transfers between devices: 17.9 us -> 0.02 us  [local(): frozen_full = lax.all_gather(frozen, DATA, axis=0, tiled=True)]
    reshape x4 -> x5, local copies, waits for them, and re-layouts: 10.3 us -> 5.56 us  [the longest x1 1.83 us: local(): swapped[:, :, :keys_here].reshape(enc_columns, HD)]
  transfers between devices with their start and end apart: 15 -> 15, of which waited for: 11 -> 8; matrix products, arithmetic and copies ran while one was open for 15% -> 15% of each run, Pallas kernels for 4% -> 5%
where the time goes in v4:
time: 508 us; the launch traced here: 505 us
  waiting for transfers between devices  229 us (45%)
  blocking collectives  92.9 us (18%)
  local copies, waits for them, and re-layouts  50.8 us (10%)
  starting transfers between devices  38.6 us (8%)
  matrix products  30.2 us (6%)
  other arithmetic  25.9 us (5%)
  Pallas kernels  23 us (5%)
  between operations  14.2 us (3%)
    ppermute x5, waiting for transfers between devices, pair_swap(): return lax.ppermute(given, 'yl', [(0, 1), (1, 0)])  101 us
    all_to_all x2, blocking collectives, scatter_sum(): lax.all_to_all(partial_rows.astype(jnp.bfloat16).reshape(size, share, par...  76.1 us
    all_to_all x1, waiting for transfers between devices, local(): lax.all_to_all(jnp.broadcast_to(class_pieces.reshape(1, 2, 1, 2 * keys_he...  58.3 us
    all_to_all x2, waiting for transfers between devices, copies_to(): lax.all_to_all(copies, axis, split_axis=0, concat_axis=0, tiled=True)  36.2 us
    all_to_all x2, waiting for transfers between devices, scatter_sum(): lax.all_to_all(partial_rows.astype(jnp.bfloat16).reshape(size, share, par...  30.3 us
    all_to_all x1, blocking collectives, local(): lax.all_to_all(requests, DATA, split_axis=0, concat_axis=0, tiled=True)  16.8 us
    unnamed x35, local copies, waits for them, and re-layouts  15.2 us
    dot_general x4, matrix products, contract_last(): lax.dot_general(left_side, right_side, (((1,), (1,)), ((), ())), preferre...  12 us
  transfers between devices with their start and end apart: 15, of which 8 were waited for; matrix products, arithmetic and copies ran while one was open for 15% of the time, Pallas kernels for 5%

profile of v4, /device:TPU:1, one launch (start us, length us, event | category | flops | bytes accessed | tf_op | source)
XLA Modules:
  0.0 505.0 jit_solution(961122458256327681)
XLA Ops:
  9.2 16.8 %all_to_all.49 = s32[16,1,2]{2,1,0:T(1,128)S(1)} all-to-all(s32[16,1,2]{2,1,0:T(1,128)S(1)} %copy.89), channel_id=1, replica_groups=mesh['z'=8,'core'=2,'yh'=2,'yl'=2,'x'=4] {'z','core'}, dimensions={0} | all-to-all | bytes 256 | tf_op jit(solution)/shard_map/all_to_all | solution.py:237
  27.3 3.2 gather_fusion
  30.5 4.8 all-to-all-start.1
  35.4 2.5 constant_dynamic-update-slice_fusion.1
  37.8 2.5 constant_dynamic-update-slice_fusion.first_weights
  46.3 1.8 pad_maximum_fusion.2
  48.1 62.6 %collective-permute-done = bf16[2,64,128]{2,1,0:T(8,128)(2,1)S(1)} collective-permute-done((bf16[2,64,128]{2,1,0:T(8,128)(2,1)S(1)}, bf16[2,64,128]{2,1,0:T(8,128)(2,1)S(1)}, u32[]{:S(2)}, u32[]{:S(2)}) %collective-permute-start) | collective-permute-done | bytes 32800 | tf_op jit(solution)/shard_map/ppermute | solution.py:90
  110.8 3.0 gather_fusion.1
  114.8 2.4 broadcast_in_dim.51
  117.2 6.8 %all-to-all-start.2 = ((bf16[16,512,256]{2,1,0:T(8,128)(2,1)}), bf16[16,512,256]{2,1,0:T(8,128)(2,1)}, u32[]{:S(2)}, u32[]{:S(2)}) async-start(bf16[16,512,256]{2,1,0:T(8,128)(2,1)} %bitcast.91), calls=%async_computation.2 | async-start | bytes 8388608 | tf_op jit(solution)/shard_map/all_to_all | solution.py:277
  124.1 3.1 pad_maximum_fusion
  127.1 58.3 %all-to-all-done.2.enc = bf16[16,512,256]{2,1,0:T(8,128)(2,1)} async-done(((bf16[16,512,256]{2,1,0:T(8,128)(2,1)}), bf16[16,512,256]{2,1,0:T(8,128)(2,1)}, u32[]{:S(2)}, u32[]{:S(2)}) %all-to-all-start.2) | async-done | bytes 4194336 | tf_op jit(solution)/shard_map/all_to_all | solution.py:277
  185.4 11.4 %shard_map.154 = bf16[2,512,256]{2,1,0:T(8,128)(2,1)S(1)} custom-call(bf16[16,512,256]{2,1,0:T(8,128)(2,1)} %all-to-all-done.2.enc, bf16[4096,256]{1,0:T(8,128)(2,1)} %constant_dynamic-update-slice_fusion.first_weights, bf16[4096,256]{1,0:T(8,128)(2,1)} %collective-permute-done.1.second_weights), custom_call_target="tpu_custom_call" | custom-call | flops 2147483648 | bytes 8388608 | tf_op jit(solution)/shard_map/pallas_call | solution.py:178
  199.2 2.0 convolution_convert_fusion.3
  201.3 19.0 %all_to_all.50 = bf16[8,16,4096]{2,1,0:T(8,128)(2,1)S(1)} all-to-all(bf16[8,16,4096]{2,1,0:T(8,128)(2,1)S(1)} %bitcast.95), channel_id=1, replica_groups=mesh['z'=8,'core'=2,'yh'=2,'yl'=2,'x'=4] {'yh','x'}, dimensions={0} | all-to-all | bytes 2097152 | tf_op jit(solution)/shard_map/all_to_all | solution.py:74
  222.4 1.6 broadcast_in_dim.52
  224.0 4.4 all-to-all-start.4
  228.5 5.0 fusion.8
  233.4 26.6 %all-to-all-done.4 = bf16[16,16,4096]{2,1,0:T(8,128)(2,1)} async-done(((bf16[16,16,4096]{2,1,0:T(8,128)(2,1)}), bf16[16,16,4096]{2,1,0:T(8,128)(2,1)}, u32[]{:S(2)}, u32[]{:S(2)}) %all-to-all-start.4) | async-done | bytes 2097184 | tf_op jit(solution)/shard_map/all_to_all | solution.py:67
  260.0 4.3 fusion.3
  266.8 57.1 %all_to_all.51 = bf16[16,16,4096]{2,1,0:T(8,128)(2,1)S(1)} all-to-all(bf16[16,16,4096]{2,1,0:T(8,128)(2,1)S(1)} %bitcast.98), channel_id=1, replica_groups=mesh['z'=8,'core'=2,'yh'=2,'yl'=2,'x'=4] {'yh','yl','x'}, dimensions={0} | all-to-all | bytes 4194304 | tf_op jit(solution)/shard_map/all_to_all | solution.py:74
  326.7 4.2 all-to-all-start.6
  330.9 1.8 fusion.56
  332.7 5.1 %convolution_convert_fusion.1 = bf16[256,4096]{1,0:T(8,128)(2,1)} fusion(bf16[4096,1024]{0,1:T(8,128)(2,1)} %all-gather.4.cloned.1.call-done, f32[256,512]{0,1:T(8,128)} %copy-done.13), kind=kOutput, calls=%fused_computation.5 | convolution fusion | flops 1075970048 | bytes 6815744 | tf_op jit(solution)/shard_map/dot_general | solution.py:53
  337.8 9.6 %all-to-all-done.6 = bf16[8,16,4096]{2,1,0:T(8,128)(2,1)} async-done(((bf16[8,16,4096]{2,1,0:T(8,128)(2,1)}), bf16[8,16,4096]{2,1,0:T(8,128)(2,1)}, u32[]{:S(2)}, u32[]{:S(2)}) %all-to-all-start.6) | async-done | bytes 1048608 | tf_op jit(solution)/shard_map/all_to_all | solution.py:67
  347.4 3.4 convolution_convert_fusion.6
  354.7 2.1 convolution_convert_fusion.4
  359.5 1.8 pad_maximum_fusion.1
  361.3 12.8 %collective-permute-done.3.grad_other = bf16[128,4096]{1,0:T(8,128)(2,1)} collective-permute-done((bf16[128,4096]{1,0:T(8,128)(2,1)}, bf16[128,4096]{1,0:T(8,128)(2,1)}, u32[]{:S(2)}, u32[]{:S(2)}) %collective-permute-start.3) | collective-permute-done | bytes 1048608 | tf_op jit(solution)/shard_map/ppermute | solution.py:90
  374.1 4.4 all-to-all-start.7
  378.6 1.7 slice.58
  380.3 1.6 collective-permute-start.4
  383.9 25.2 %collective-permute-done.4 = bf16[2,640,128]{2,1,0:T(8,128)(2,1)} collective-permute-done((bf16[2,640,128]{2,1,0:T(8,128)(2,1)}, bf16[2,640,128]{2,1,0:T(8,128)(2,1)}, u32[]{:S(2)}, u32[]{:S(2)}) %collective-permute-start.4) | collective-permute-done | bytes 327712 | tf_op jit(solution)/shard_map/ppermute | solution.py:90
  410.9 1.8 copy.102
  412.8 1.8 reshape.178
  414.6 1.8 copy.103
  416.4 1.8 reshape.179
  423.2 3.4 copy-done.1
  426.5 11.6 %shard_map.155 = (bf16[8,256,512]{2,1,0:T(8,128)(2,1)S(1)}, bf16[8,256,512]{2,1,0:T(8,128)(2,1)S(1)}) custom-call(s32[1]{0:T(128)} %bitcast.20.core, bf16[16,1024,256]{2,1,0:T(8,128)(2,1)S(1)} %bitcast.83, bf16[256,4096]{1,0:T(8,128)(2,1)S(1)} %fusion.1.normed, bf16[128,4096]{1,0:T(8,128)(2,1)} %bitcast.24.grad_own, ...), custom_call_target="tpu_custom_call" | custom-call | flops 2684354560 | bytes 16777216 | tf_op jit(solution)/shard_map/pallas_call | solution.py:128
  440.8 2.7 convert_reduce_fusion.1
  443.5 2.7 collective-permute-start.5
  446.2 4.0 collective-permute-done.5
  450.2 1.9 add_convert_fusion
  453.0 2.0 convolution_convert_fusion
  455.0 5.7 %all-to-all-start.8 = ((bf16[16,16,4096]{2,1,0:T(8,128)(2,1)}), bf16[16,16,4096]{2,1,0:T(8,128)(2,1)S(1)}, u32[]{:S(2)}, u32[]{:S(2)}) async-start(bf16[16,16,4096]{2,1,0:T(8,128)(2,1)} %bitcast.92), calls=%async_computation.8 | async-start | bytes 4194304 | tf_op jit(solution)/shard_map/all_to_all | solution.py:74
  460.9 1.6 fusion.39
  462.5 30.3 %all-to-all-done.8 = bf16[16,16,4096]{2,1,0:T(8,128)(2,1)S(1)} async-done(((bf16[16,16,4096]{2,1,0:T(8,128)(2,1)}), bf16[16,16,4096]{2,1,0:T(8,128)(2,1)S(1)}, u32[]{:S(2)}, u32[]{:S(2)}) %all-to-all-start.8) | async-done | bytes 2097184 | tf_op jit(solution)/shard_map/all_to_all | solution.py:74
  496.0 1.7 fusion.31
  (109 shorter events, 43.0 us)
Async XLA Ops:
  7.2 35.7 %copy-start = (bf16[4096,128]{1,0:T(8,128)(2,1)S(1)}, bf16[4096,128]{1,0:T(8,128)(2,1)}, u32[]{:S(2)}) copy-start(bf16[4096,128]{1,0:T(8,128)(2,1)} %param.15) | copy-start | bytes 3145732
  30.5 80.3 %all-to-all-start.1 = ((bf16[16,2,128,256]{3,2,1,0:T(8,128)(2,1)}), bf16[16,2,128,256]{3,2,1,0:T(8,128)(2,1)}, u32[]{:S(2)}, u32[]{:S(2)}) async-start(bf16[16,2,128,256]{3,2,1,0:T(8,128)(2,1)} %bitcast.1), calls=%async_computation.1 | async-start | bytes 4194304 | tf_op jit(solution)/shard_map/all_to_all | solution.py:238
  35.3 6.5 %copy-start.6 = (bf16[256,4096]{1,0:T(8,128)(2,1)S(1)}, bf16[256,4096]{1,0:T(8,128)(2,1)}, u32[]{:S(2)}) copy-start(bf16[256,4096]{1,0:T(8,128)(2,1)} %param.11) | copy-start | bytes 6291460
  35.3 193.1 %all-gather.4.cloned.1.call-start = ((), (), s32[]{:S(2)}) async-start(), calls=%async_computation.10 | async-start | bytes 8912896 | tf_op jit(solution)/shard_map/all_gather | solution.py:290
  37.8 4.5 copy-start.7
  40.3 73.4 %collective-permute-start.1 = (bf16[4096,256]{1,0:T(8,128)(2,1)}, bf16[4096,256]{1,0:T(8,128)(2,1)}, u32[]{:S(2)}, u32[]{:S(2)}) collective-permute-start(bf16[4096,256]{1,0:T(8,128)(2,1)} %constant_dynamic-update-slice_fusion.first_weights), channel_id=1, source_target_pairs={{0,4},{4,0},{1,5},{5,1},{2,6},{6,2},{3,7},{7,3},{8,12},{12,8},{9,1... | collective-permute-start | bytes 6291464 | tf_op jit(solution)/shard_map/ppermute | solution.py:90
  41.6 72.1 %collective-permute-start.2 = (bf16[128,4096]{1,0:T(8,128)(2,1)}, bf16[128,4096]{1,0:T(8,128)(2,1)}, u32[]{:S(2)}, u32[]{:S(2)}) collective-permute-start(bf16[128,4096]{1,0:T(8,128)(2,1)} %param.18), channel_id=1, source_target_pairs={{0,4},{4,0},{1,5},{5,1},{2,6},{6,2},{3,7},{7,3},{8,12},{12,8},{9,1... | collective-permute-start | bytes 3145736 | tf_op jit(solution)/shard_map/ppermute | solution.py:90
  42.9 2.1 copy-start.11
  43.6 67.1 %collective-permute-start = (bf16[2,64,128]{2,1,0:T(8,128)(2,1)S(1)}, bf16[2,64,128]{2,1,0:T(8,128)(2,1)S(1)}, u32[]{:S(2)}, u32[]{:S(2)}) collective-permute-start(bf16[2,64,128]{2,1,0:T(8,128)(2,1)S(1)} %get-tuple-element.99), channel_id=1, source_target_pairs={{0,4},{4,0},{1,5},{5,1},{2,6},{6,2},{3,7},{7,3},{8,12},{12,8},{9,1... | collective-permute-start | bytes 98312 | tf_op jit(solution)/shard_map/ppermute | solution.py:90
  117.2 68.2 %all-to-all-start.2 = ((bf16[16,512,256]{2,1,0:T(8,128)(2,1)}), bf16[16,512,256]{2,1,0:T(8,128)(2,1)}, u32[]{:S(2)}, u32[]{:S(2)}) async-start(bf16[16,512,256]{2,1,0:T(8,128)(2,1)} %bitcast.91), calls=%async_computation.2 | async-start | bytes 8388608 | tf_op jit(solution)/shard_map/all_to_all | solution.py:277
  124.0 223.4 %all-gather.6.cloned.1.call-start = ((), (), s32[]{:S(2)}) async-start(), calls=%async_computation.12 | async-start | bytes 8912896 | tf_op jit(solution)/shard_map/all_gather | solution.py:316
  196.8 0.8 copy-start.2
  197.9 3.4 copy-start.10
  224.0 36.0 %all-to-all-start.4 = ((bf16[16,16,4096]{2,1,0:T(8,128)(2,1)}), bf16[16,16,4096]{2,1,0:T(8,128)(2,1)}, u32[]{:S(2)}, u32[]{:S(2)}) async-start(bf16[16,16,4096]{2,1,0:T(8,128)(2,1)} %broadcast_in_dim.52), calls=%async_computation.4 | async-start | bytes 4194304 | tf_op jit(solution)/shard_map/all_to_all | solution.py:67
  260.0 5.2 %copy-start.12 = (bf16[4096,1024]{0,1:T(8,128)(2,1)S(1)}, bf16[4096,1024]{0,1:T(8,128)(2,1)}, u32[]{:S(2)}) copy-start(bf16[4096,1024]{0,1:T(8,128)(2,1)} %all-gather.4.cloned.1.call-done) | copy-start | bytes 25165828
  260.0 5.3 %copy-start.14 = (f32[256,512]{0,1:T(8,128)S(1)}, f32[256,512]{0,1:T(8,128)}, u32[]{:S(2)}) copy-start(f32[256,512]{0,1:T(8,128)} %fusion.8) | copy-start | bytes 1572868
  265.3 1.5 copy-start.13
  326.7 20.7 %all-to-all-start.6 = ((bf16[8,16,4096]{2,1,0:T(8,128)(2,1)}), bf16[8,16,4096]{2,1,0:T(8,128)(2,1)}, u32[]{:S(2)}, u32[]{:S(2)}) async-start(bf16[8,16,4096]{2,1,0:T(8,128)(2,1)} %broadcast_in_dim.53), calls=%async_computation.6 | async-start | bytes 2097152 | tf_op jit(solution)/shard_map/all_to_all | solution.py:67
  350.8 23.3 %collective-permute-start.3 = (bf16[128,4096]{1,0:T(8,128)(2,1)}, bf16[128,4096]{1,0:T(8,128)(2,1)}, u32[]{:S(2)}, u32[]{:S(2)}) collective-permute-start(bf16[128,4096]{1,0:T(8,128)(2,1)} %bitcast.24.grad_own), channel_id=1, source_target_pairs={{0,4},{4,0},{1,5},{5,1},{2,6},{6,2},{3,7},{7,3},{8,12},{12,8},{9,1... | collective-permute-start | bytes 3145736 | tf_op jit(solution)/shard_map/ppermute | solution.py:90
  353.9 0.6 copy-start.9
  374.1 66.7 %all-to-all-start.7 = ((bf16[16,16,4096]{2,1,0:T(8,128)(2,1)}), bf16[16,16,4096]{2,1,0:T(8,128)(2,1)}, u32[]{:S(2)}, u32[]{:S(2)}) async-start(bf16[16,16,4096]{2,1,0:T(8,128)(2,1)} %bitcast.97), calls=%async_computation.7 | async-start | bytes 4194304 | tf_op jit(solution)/shard_map/all_to_all | solution.py:74
  378.5 114.6 %reduce-scatter.2.cloned.1.call-start = ((), (), s32[]{:S(2)}) async-start(), calls=%async_computation.11 | async-start | bytes 2359296 | tf_op jit(solution)/shard_map/reduce_scatter | solution.py:202
  380.3 28.7 %collective-permute-start.4 = (bf16[2,640,128]{2,1,0:T(8,128)(2,1)}, bf16[2,640,128]{2,1,0:T(8,128)(2,1)}, u32[]{:S(2)}, u32[]{:S(2)}) collective-permute-start(bf16[2,640,128]{2,1,0:T(8,128)(2,1)} %slice.58), channel_id=1, source_target_pairs={{0,4},{4,0},{1,5},{5,1},{2,6},{6,2},{3,7},{7,3},{8,12},{12,8},{9,1... | collective-permute-start | bytes 983048 | tf_op jit(solution)/shard_map/ppermute | solution.py:90
  423.2 3.4 copy-start.1
  438.1 1.3 copy-start.3
  439.4 1.4 copy-start.5
  440.8 9.5 %copy-start.4 = (bf16[8,256,512]{2,1,0:T(8,128)(2,1)S(1)}, bf16[8,256,512]{2,1,0:T(8,128)(2,1)}, u32[]{:S(2)}) copy-start(bf16[8,256,512]{2,1,0:T(8,128)(2,1)} %copy-done.3) | copy-start | bytes 6291460
  443.5 6.7 %collective-permute-start.5 = (bf16[8,256,512]{2,1,0:T(8,128)(2,1)}, bf16[8,256,512]{2,1,0:T(8,128)(2,1)S(1)}, u32[]{:S(2)}, u32[]{:S(2)}) collective-permute-start(bf16[8,256,512]{2,1,0:T(8,128)(2,1)} %copy-done.5), channel_id=1, source_target_pairs={{0,16},{16,0},{1,17},{17,1},{2,18},{18,2},{3,19},{19,3},{4,20},{20... | collective-permute-start | bytes 6291464 | tf_op jit(solution)/shard_map/ppermute | solution.py:199
  452.2 0.8 copy-start.8
  455.0 37.8 %all-to-all-start.8 = ((bf16[16,16,4096]{2,1,0:T(8,128)(2,1)}), bf16[16,16,4096]{2,1,0:T(8,128)(2,1)S(1)}, u32[]{:S(2)}, u32[]{:S(2)}) async-start(bf16[16,16,4096]{2,1,0:T(8,128)(2,1)} %bitcast.92), calls=%async_computation.8 | async-start | bytes 4194304 | tf_op jit(solution)/shard_map/all_to_all | solution.py:74
Sparse Core Ops, SparseCore 0:
  113.9 67.2 all-gather.3
  221.3 113.6 all-gather.5
  452.3 37.9 reduce-scatter.1
